TPU v7x, 256 devices: a whole 4x4x8 slice. The times are simulated.
256 devices in a mesh: fsdp: 32 (over x, y, core), tp: 8 (over z).
Axes of the slice: x: 4, y: 4, z: 8, core: 2. Of those that a mesh axis runs over, the one named last changes fastest.
Arguments:
- momentum: bfloat16 [2, 28672, 8192], P(None, 'fsdp', 'tp'), may hold values from -200 to 200
- right_factor: bfloat16 [2, 512, 8192], P(None, 'fsdp', 'tp'), may hold values from -6 to 6
Outputs:
- new_momentum: bfloat16 [2, 28672, 8192], P(None, 'fsdp', 'tp')
- update: bfloat16 [2, 28672, 8192], P(None, 'fsdp', 'tp')
- new_factor: bfloat16 [2, 512, 8192], P(None, 'fsdp', 'tp')
All inputs are finite; a program needn't handle non-finite values.
Results may differ from a plain program's by a relative error of at most 0.006.
Values may be sent and summed in bfloat16 or wider, within the bound.
A program may use at most 128 MiB of HBM per device.

v0:
```python
import math

import jax
import jax.numpy as jnp
from jax import lax
from jax.sharding import PartitionSpec as P

D = 8192
FF = 28672
RANK = 512


def invert_gram(gram):
    chol = jnp.linalg.cholesky(gram)
    identity = jnp.broadcast_to(jnp.eye(gram.shape[-1], dtype=jnp.float32), gram.shape)
    return lax.linalg.triangular_solve(chol, identity, left_side=True, lower=True)


def orthonormalize(project, inverse):
    return jnp.einsum("lrk,ljk->lrj", project, inverse, precision=lax.Precision.HIGHEST).astype(
        jnp.bfloat16
    )


def dion_layers(momentum, factor):
    highest = lax.Precision.HIGHEST
    partial_sums = jnp.einsum(
        "lrd,lkd->lrk",
        momentum,
        lax.all_gather(factor, "fsdp", axis=1, tiled=True),
        preferred_element_type=jnp.float32,
    )
    project = lax.psum(partial_sums, "tp")
    local_gram = jnp.einsum("lrk,lrj->lkj", project, project, precision=highest)
    gram = lax.psum(local_gram, "fsdp")
    ortho = orthonormalize(project, invert_gram(gram))
    right = lax.psum_scatter(
        jnp.einsum("lrk,lrd->kld", ortho, momentum, preferred_element_type=jnp.float32),
        "fsdp",
        scatter_dimension=0,
        tiled=True,
    )
    sumsq = lax.psum(jnp.sum(right * right, axis=2), "tp")
    normed = (right * lax.rsqrt(sumsq + 1e-06)[:, :, None]).astype(jnp.bfloat16)
    right_b = right.astype(jnp.bfloat16)
    whole_right, whole_normed = (
        lax.all_gather(right_b, "fsdp", axis=0, tiled=True),
        lax.all_gather(normed, "fsdp", axis=0, tiled=True),
    )
    feedback = jnp.einsum("lrk,kld->lrd", ortho, whole_right, preferred_element_type=jnp.float32)
    direction = jnp.einsum("lrk,kld->lrd", ortho, whole_normed, preferred_element_type=jnp.float32)
    scale = math.sqrt(FF * D / RANK)
    new_mom = (momentum.astype(jnp.float32) - 0.05 * feedback).astype(jnp.bfloat16)
    update = (scale * direction).astype(jnp.bfloat16)
    return (new_mom, update, jnp.transpose(normed, (1, 0, 2)))


def local(momentum, right_factor):
    results = []
    for layer in range(momentum.shape[0]):
        results.append(dion_layers(momentum[layer : layer + 1], right_factor[layer : layer + 1]))
    new_mom = jnp.concatenate([item[0] for item in results], axis=0)
    update = jnp.concatenate([item[1] for item in results], axis=0)
    new_fac = jnp.concatenate([item[2] for item in results], axis=0)
    return (new_mom, update, new_fac)


def solution(mesh):
    return jax.shard_map(
        local,
        mesh=mesh,
        in_specs=(P(None, "fsdp", "tp"), P(None, "fsdp", "tp")),
        out_specs=(P(None, "fsdp", "tp"), P(None, "fsdp", "tp"), P(None, "fsdp", "tp")),
        check_vma=False,
    )
```

profile of v0, /device:TPU:1, one launch (start us, length us, event | category | flops | bytes accessed | tf_op | source)
XLA Modules:
  0.0 1008.4 jit_solution(16650413647950012806)
XLA Ops:
  9.4 53.7 %all-gather.11.cloned.1.call-done = bf16[1,512,1024]{2,1,0:T(8,128)(2,1)} async-done(((bf16[1,16,1024]{2,1,0:T(8,128)(2,1)}), bf16[1,512,1024]{2,1,0:T(8,128)(2,1)}) %all-gather.11.cloned.1.call-update) | async-done | bytes 1048592 | tf_op jit(solution)/shard_map/all_gather | solution.py:30
  63.2 4.2 fusion.4
  67.3 46.2 %all-gather.7.cloned.1.call-done = bf16[1,512,1024]{2,1,0:T(8,128)(2,1)} async-done(((bf16[1,16,1024]{2,1,0:T(8,128)(2,1)}), bf16[1,512,1024]{2,1,0:T(8,128)(2,1)}) %all-gather.7.cloned.1.call-update) | async-done | bytes 1048592 | tf_op jit(solution)/shard_map/all_gather | solution.py:30
  113.5 4.2 fusion.8
  117.8 98.9 %all-reduce.9.cloned.1.call-done = (f32[896,512]{1,0:T(8,128)}, f32[896,512]{1,0:T(8,128)}) async-done(((f32[896,512]{1,0:T(8,128)}, f32[896,512]{1,0:T(8,128)}), (f32[896,512]{1,0:T(8,128)}, f32[896,512]{1,0:T(8,128)})) %all-reduce.9.cloned.1.call-update) | async-done | bytes 3670032 | tf_op jit(solution)/shard_map/psum | solution.py:33
  216.6 6.7 convolution_bitcast_fusion
  223.3 4.5 convolution_bitcast_fusion.1
  228.5 115.7 %all-reduce.7.cloned.1.call-done = (f32[1,512,512]{1,2,0:T(8,128)}, f32[1,512,512]{1,2,0:T(8,128)}) async-done(((f32[1,512,512]{1,2,0:T(8,128)}, f32[1,512,512]{1,2,0:T(8,128)}), (f32[1,512,512]{1,2,0:T(8,128)}, f32[1,512,512]{1,2,0:T(8,128)})) %all-reduce.7.cloned.1.call-update) | async-done | bytes 2097168 | tf_op jit(solution)/shard_map/psum | solution.py:35
  344.2 2.5 copy.8
  346.8 2.5 copy.6
  349.3 3.6 fusion.59
  353.9 11.7 %custom-call.43 = f32[1,128,128]{2,1,0:T(8,128)S(1)} custom-call(f32[1,128,128]{2,1,0:T(8,128)S(1)} %cholesky.438), custom_call_target="Cholesky" | custom-call | tf_op jit(solution)/shard_map/jit(cholesky)/cholesky | solution.py:14
  366.5 11.7 %custom-call.35 = f32[1,128,128]{2,1,0:T(8,128)S(1)} custom-call(f32[1,128,128]{2,1,0:T(8,128)S(1)} %cholesky.425), custom_call_target="Cholesky" | custom-call | tf_op jit(solution)/shard_map/jit(cholesky)/cholesky | solution.py:14
  378.9 9.8 custom-call.36
  389.4 9.9 custom-call.44
  403.7 11.7 %custom-call.45 = f32[1,128,128]{2,1,0:T(8,128)S(1)} custom-call(f32[1,128,128]{2,1,0:T(8,128)S(1)} %cholesky.442), custom_call_target="Cholesky" | custom-call | tf_op jit(solution)/shard_map/jit(cholesky)/cholesky | solution.py:14
  416.7 9.8 custom-call.46
  428.9 11.9 %custom-call.47 = f32[1,128,128]{2,1,0:T(8,128)S(1)} custom-call(f32[1,128,128]{2,1,0:T(8,128)S(1)} %cholesky.447), custom_call_target="Cholesky" | custom-call | tf_op jit(solution)/shard_map/jit(cholesky)/cholesky | solution.py:14
  442.1 9.8 custom-call.48
  454.2 11.7 %custom-call.49 = f32[1,128,128]{2,1,0:T(8,128)S(1)} custom-call(f32[1,128,128]{2,1,0:T(8,128)S(1)} %fusion.43), custom_call_target="Cholesky" | custom-call | tf_op jit(solution)/shard_map/jit(cholesky)/cholesky | solution.py:14
  471.5 11.7 %custom-call.37 = f32[1,128,128]{2,1,0:T(8,128)S(1)} custom-call(f32[1,128,128]{2,1,0:T(8,128)S(1)} %cholesky.429), custom_call_target="Cholesky" | custom-call | tf_op jit(solution)/shard_map/jit(cholesky)/cholesky | solution.py:14
  484.5 10.2 %custom-call.38 = f32[1,1,128,128]{2,3,1,0:T(8,128)S(1)} custom-call(f32[1,1,128,128]{3,2,1,0:T(8,128)S(1)} %get-tuple-element.57), custom_call_target="InvertDiagBlocksLowerTriangular" | custom-call | tf_op jit(solution)/shard_map/jit(cholesky)/cholesky | solution.py:14
  497.1 11.7 %custom-call.39 = f32[1,128,128]{2,1,0:T(8,128)S(1)} custom-call(f32[1,128,128]{2,1,0:T(8,128)S(1)} %cholesky.434), custom_call_target="Cholesky" | custom-call | tf_op jit(solution)/shard_map/jit(cholesky)/cholesky | solution.py:14
  510.1 9.8 custom-call.40
  522.2 11.7 %custom-call.41 = f32[1,128,128]{2,1,0:T(8,128)S(1)} custom-call(f32[1,128,128]{2,1,0:T(8,128)S(1)} %fusion.42), custom_call_target="Cholesky" | custom-call | tf_op jit(solution)/shard_map/jit(cholesky)/cholesky | solution.py:14
  537.8 2.3 select_select_fusion.1
  540.1 11.9 %while.4 = (s32[]{:T(128)}, f32[1,512,512]{2,1,0:T(8,128)}, s32[4,2]{0,1:T(2,128)S(1)}, f32[4,1,128,128]{3,2,1,0:T(8,128)S(1)}, s32[]{:T(128)}) while((s32[]{:T(128)}, f32[1,512,512]{2,1,0:T(8,128)}, s32[4,2]{0,1:T(2,128)S(1)}, f32[4,1,128,128]{3,2,1,0:T(8,128)S(1)}, s32[]{:T(128)}) %tuple.61), condition=%wide.while_cond, body=%wide.while_body.sunk | while | flops 2 | bytes 131189 | solution.py:16
  540.8 2.3 bitcast_dynamic-update-slice_fusion.4
  543.8 2.3 bitcast_dynamic-update-slice_fusion.4
  546.8 2.3 bitcast_dynamic-update-slice_fusion.4
  552.1 39.3 %custom-call.42 = f32[1,4,128,128]{2,3,1,0:T(8,128)S(1)} custom-call(f32[1,4,128,128]{3,2,1,0:T(8,128)S(1)} %bitcast.382), custom_call_target="InvertDiagBlocksLowerTriangular" | custom-call | tf_op jit(solution)/shard_map/triangular_solve/custom-call.3 | solution.py:16
  597.2 3.1 convolution_convert_fusion.1
  601.2 2.6 fusion.10
  607.9 7.7 while.5
  615.7 39.3 %custom-call.50 = f32[1,4,128,128]{2,3,1,0:T(8,128)S(1)} custom-call(f32[1,4,128,128]{3,2,1,0:T(8,128)S(1)} %bitcast.381), custom_call_target="InvertDiagBlocksLowerTriangular" | custom-call | tf_op jit(solution)/shard_map/triangular_solve/custom-call.3 | solution.py:16
  658.2 3.1 convolution_convert_fusion
  662.2 2.6 fusion.13
  664.9 24.3 %reduce-scatter.3.cloned.1.call-done = f32[16,1,1024]{2,0,1:T(8,128)} async-done(((f32[512,1,1024]{2,0,1:T(8,128)}), f32[16,1,1024]{2,0,1:T(8,128)}) %reduce-scatter.3.cloned.1.call-update) | async-done | bytes 65552 | tf_op jit(solution)/shard_map/reduce_scatter | solution.py:37
  690.1 89.3 %reduce-scatter.5.cloned.1.call-done = f32[16,1,1024]{2,0,1:T(8,128)} async-done(((f32[512,1,1024]{2,0,1:T(8,128)}), f32[16,1,1024]{2,0,1:T(8,128)}) %reduce-scatter.5.cloned.1.call-update) | async-done | bytes 65552 | tf_op jit(solution)/shard_map/reduce_scatter | solution.py:37
  780.4 13.7 %all-reduce.2 = (f32[16,1]{0,1:T(1,128)S(1)}, f32[16,1]{0,1:T(1,128)S(1)}) all-reduce(f32[16,1]{0,1:T(1,128)S(1)} %bitcast.384, f32[16,1]{0,1:T(1,128)S(1)} %bitcast.383), channel_id=1, replica_groups=mesh['fsdp'=32,'tp'=8] {'tp'}, use_global_device_ids=true, to_apply=%region_17.20 | all-reduce | flops 32 | bytes 256 | tf_op jit(solution)/shard_map/psum | solution.py:43
  800.1 46.1 %all-gather.9.cloned.1.call-done = bf16[512,1,1024]{2,0,1:T(8,128)(2,1)} async-done(((bf16[16,1,1024]{2,0,1:T(8,128)(2,1)}), bf16[512,1,1024]{2,0,1:T(8,128)(2,1)}) %all-gather.9.cloned.1.call-update) | async-done | bytes 1048592 | tf_op jit(solution)/shard_map/all_gather | solution.py:47
  846.2 2.9 fusion.1
  849.1 47.4 %all-gather.13.cloned.1.call-done = bf16[512,1,1024]{2,0,1:T(8,128)(2,1)} async-done(((bf16[16,1,1024]{2,0,1:T(8,128)(2,1)}), bf16[512,1,1024]{2,0,1:T(8,128)(2,1)}) %all-gather.13.cloned.1.call-update) | async-done | bytes 1048592 | tf_op jit(solution)/shard_map/all_gather | solution.py:47
  896.5 3.2 fusion
  901.9 44.4 %all-gather.15.cloned.1.call-done = bf16[512,1,1024]{2,0,1:T(8,128)(2,1)} async-done(((bf16[16,1,1024]{2,0,1:T(8,128)(2,1)}), bf16[512,1,1024]{2,0,1:T(8,128)(2,1)}) %all-gather.15.cloned.1.call-update) | async-done | bytes 1048592 | tf_op jit(solution)/shard_map/all_gather | solution.py:48
  946.3 2.3 fusion.16
  948.6 47.9 %all-gather.17.cloned.1.call-done = bf16[512,1,1024]{2,0,1:T(8,128)(2,1)} async-done(((bf16[16,1,1024]{2,0,1:T(8,128)(2,1)}), bf16[512,1,1024]{2,0,1:T(8,128)(2,1)}) %all-gather.17.cloned.1.call-update) | async-done | bytes 1048592 | tf_op jit(solution)/shard_map/all_gather | solution.py:48
  996.5 2.6 fusion.17
  (123 shorter events, 69.1 us)
Async XLA Ops:
  7.2 56.0 %all-gather.11.cloned.1.call-start = ((), (), s32[]{:S(2)}) async-start(), calls=%async_computation.5 | async-start | bytes 1081344 | tf_op jit(solution)/shard_map/all_gather | solution.py:30
  8.6 104.9 %all-gather.7.cloned.1.call-start = ((), (), s32[]{:S(2)}) async-start(), calls=%async_computation.2 | async-start | bytes 1081344 | tf_op jit(solution)/shard_map/all_gather | solution.py:30
  9.4 207.2 %all-reduce.9.cloned.1.call-start = ((), (), s32[]{:S(2)}) async-start(), calls=%async_computation.11 | async-start | bytes 7340032 | tf_op jit(solution)/shard_map/psum | solution.py:33
  117.7 226.5 %all-reduce.7.cloned.1.call-start = ((), (), s32[]{:S(2)}) async-start(), calls=%async_computation.10 | async-start | bytes 4194304 | tf_op jit(solution)/shard_map/psum | solution.py:35
  216.6 6.7 copy-start.1
  227.8 461.3 %reduce-scatter.3.cloned.1.call-start = ((), (), s32[]{:S(2)}) async-start(), calls=%async_computation.3 | async-start | bytes 2162688 | tf_op jit(solution)/shard_map/reduce_scatter | solution.py:37
  352.9 1.0 copy-start.2
  597.2 4.0 copy-start.6
  600.3 0.9 copy-start.3
  603.8 175.6 %reduce-scatter.5.cloned.1.call-start = ((), (), s32[]{:S(2)}) async-start(), calls=%async_computation.6 | async-start | bytes 2162688 | tf_op jit(solution)/shard_map/reduce_scatter | solution.py:37
  656.2 1.9 copy-start
  658.2 4.0 copy-start.7
  661.3 1.0 copy-start.5
  664.8 181.4 %copy-start.4 = (bf16[896,512]{1,0:T(8,128)(2,1)S(1)}, bf16[896,512]{1,0:T(8,128)(2,1)}, u32[]{:S(2)}) copy-start(bf16[896,512]{1,0:T(8,128)(2,1)} %copy-done.3) | copy-start | bytes 2752516
  664.8 181.4 %all-gather.9.cloned.1.call-start = ((), (), s32[]{:S(2)}) async-start(), calls=%async_computation.4 | async-start | bytes 1081344 | tf_op jit(solution)/shard_map/all_gather | solution.py:47
  795.7 100.8 %all-gather.13.cloned.1.call-start = ((), (), s32[]{:S(2)}) async-start(), calls=%async_computation.7 | async-start | bytes 1081344 | tf_op jit(solution)/shard_map/all_gather | solution.py:47
  797.4 148.9 %all-gather.15.cloned.1.call-start = ((), (), s32[]{:S(2)}) async-start(), calls=%async_computation.8 | async-start | bytes 1081344 | tf_op jit(solution)/shard_map/all_gather | solution.py:48
  798.1 198.4 %all-gather.17.cloned.1.call-start = ((), (), s32[]{:S(2)}) async-start(), calls=%async_computation.9 | async-start | bytes 1081344 | tf_op jit(solution)/shard_map/all_gather | solution.py:48
Sparse Core Ops, SparseCore 0:
  11.1 52.0 all-gather.10
  66.3 47.1 all-gather.6
  117.8 98.7 all-reduce.8
  227.9 116.2 all-reduce.6
  604.0 85.1 reduce-scatter.2
  693.4 85.9 reduce-scatter.4
  795.8 50.3 all-gather.8
  849.3 47.1 all-gather.12
  899.1 47.1 all-gather.14
  949.3 47.1 all-gather.16
where the time goes:
time: 1020 us; the launch traced here: 1010 us
  waiting for transfers between devices  616 us (60%)
  other arithmetic  259 us (25%)
  matrix products  66.3 us (6%)
  local copies, waits for them, and re-layouts  31.9 us (3%)
  between operations  19.9 us (2%)
  blocking collectives  13.7 us (1%)
    another operation x30, other arithmetic, invert_gram(): chol = jnp.linalg.cholesky(gram)  162 us
    psum x1, waiting for transfers between devices, dion_layers(): gram = lax.psum(local_gram, 'fsdp')  116 us
    reduce_scatter x2, waiting for transfers between devices, dion_layers(): lax.psum_scatter(jnp.einsum('lrk,lrd->kld', ortho, momentum, preferred_el...  114 us
    all_gather x2, waiting for transfers between devices, dion_layers(): lax.all_gather(factor, 'fsdp', axis=1, tiled=True)  99.9 us
    psum x1, waiting for transfers between devices, dion_layers(): project = lax.psum(partial_sums, 'tp')  98.9 us
    all_gather x2, waiting for transfers between devices, dion_layers(): lax.all_gather(right_b, 'fsdp', axis=0, tiled=True)  93.5 us
    all_gather x2, waiting for transfers between devices, dion_layers(): lax.all_gather(normed, 'fsdp', axis=0, tiled=True)  92.2 us
    another operation x5, other arithmetic, invert_gram(): lax.linalg.triangular_solve(chol, identity, left_side=True, lower=True)  82.3 us
  transfers between devices with their start and end apart: 10, of which 10 were waited for; matrix products, arithmetic and copies ran while one was open for 8% of the time, Pallas kernels for 0%

commit v1 on v0

v1 whole, which is shorter than its diff:
```python
import functools
import math

import jax
import jax.numpy as jnp
from jax import lax
from jax.experimental import pallas as pl
from jax.experimental.pallas import tpu as pltpu
from jax.sharding import PartitionSpec as P

MESH = pl.DeviceIdType.MESH
HI = lax.Precision.HIGHEST
CORES = 2
NB = 128
VMEM_BYTES = 56 * 2**20
F32 = jnp.float32
BF16 = jnp.bfloat16


class Place:
    def __init__(self, side, depth):
        f, self.z = lax.axis_index("fsdp"), lax.axis_index("tp")
        self.side, self.depth = side, depth
        self.x, self.y, self.c = f // (side * CORES), (f // CORES) % side, f % CORES

    def at(self, x=None, y=None, c=None, z=None):
        x = self.x if x is None else x
        y = self.y if y is None else y
        c = self.c if c is None else c
        z = self.z if z is None else z
        return ((x * self.side + y) * CORES + c, z)

    def along(self, axis, t):
        return self.at(x=t) if axis == 0 else self.at(y=t)

    def mine(self, axis):
        return self.x if axis == 0 else self.y

    def others(self, axis):
        return [(o, lax.rem(self.mine(axis) + o, self.side)) for o in range(1, self.side)]

    def others_z(self):
        return [(o, lax.rem(self.z + o, self.depth)) for o in range(1, self.depth)]

    def barrier(self):
        sem = pltpu.get_barrier_semaphore()
        devices = [self.at(c=1 - self.c)]
        devices += [self.along(a, t) for a in (0, 1) for _, t in self.others(a)]
        devices += [self.at(z=t) for _, t in self.others_z()]
        for device in devices:
            pl.semaphore_signal(sem, inc=1, device_id=device, device_id_type=MESH)
        pl.semaphore_wait(sem, len(devices))


class Wire:
    def __init__(self, send, recv):
        self.send, self.recv, self.used, self.copies = send, recv, 0, []

    def put(self, src, dst, device):
        n = self.used
        self.used += 1
        copy = pltpu.make_async_remote_copy(
            src_ref=src,
            dst_ref=dst,
            send_sem=self.send.at[n],
            recv_sem=self.recv.at[n],
            device_id=device,
            device_id_type=MESH,
        )
        copy.start()
        self.copies.append(copy)
        return copy

    def finish(self):
        for copy in self.copies:
            copy.wait_send()


def arrive(copies):
    for copy in copies:
        copy.wait_recv()


def hops(depth, layer):
    far, near = depth // 2, depth - 1 - depth // 2
    return (far, near) if layer % 2 == 0 else (near, far)


def power_kernel(layers, side, depth, q_ref, m_ref, p_ref, g_ref, qall, part, chain, gpart, gcore, a_ref, s1, b_ref, s2, c_ref, s3, d_ref, send, recv):
    me = Place(side, depth)
    wire = Wire(send, recv)
    x, y, c, z = me.x, me.y, me.c, me.z
    rank = g_ref.shape[-1]
    me.barrier()

    qall[:, x, y, c] = q_ref[...]
    first = [
        [wire.put(qall.at[l, x, y, c], qall.at[l, x, y, c], me.along(l, t)) for _, t in me.others(l)]
        for l in range(layers)
    ]
    second = []
    for l in range(layers):
        arrive(first[l])
        block = qall.at[l, :, y, c] if l == 0 else qall.at[l, x, :, c]
        second.append([wire.put(block, block, me.along(1 - l, t)) for _, t in me.others(1 - l)])
    third = []
    for l in range(layers):
        arrive(second[l])
        third.append(wire.put(qall.at[l, :, :, c], qall.at[l, :, :, c], me.at(c=1 - c)))

    right, left = lax.rem(z + 1, depth), lax.rem(z + depth - 1, depth)
    rows = part.shape[2]

    def chain_step(l, way, s):
        count = hops(depth, l)[way]
        ahead = count - s + 1
        dest = lax.rem(z + ahead, depth) if way == 0 else lax.rem(z + depth - ahead, depth)
        src = part.at[l, dest]
        if s > 1:
            src = chain.at[l, way, s - 2]
            src[...] += part[l, dest]
        return wire.put(src, chain.at[l, way, s - 1], me.at(z=right if way == 0 else left))

    pending = {}
    for l in range(layers):
        third[l].wait_recv()
        factor = qall[l].reshape(rank, -1)

        @pl.loop(0, depth // 2)
        def _(i):
            lhs = m_ref[l, pl.ds(pl.multiple_of(i * 2 * rows, 16), 2 * rows), :]
            out = lax.dot_general(lhs, factor, (((1,), (1,)), ((), ())), preferred_element_type=F32)
            part[l, pl.ds(2 * i, 2)] = out.reshape(2, rows, rank)

        for way in (0, 1):
            if hops(depth, l)[way]:
                pending[l, way] = chain_step(l, way, 1)
    for s in range(2, depth // 2 + 1):
        for l in range(layers):
            for way in (0, 1):
                if s <= hops(depth, l)[way]:
                    pending[l, way].wait_recv()
                    pending[l, way] = chain_step(l, way, s)
    for l in range(layers):
        total = part[l, z]
        for way in (0, 1):
            count = hops(depth, l)[way]
            if count:
                pending[l, way].wait_recv()
                total = total + chain[l, way, count - 1]
        p_ref[l] = total
        gram = lax.dot_general(total, total, (((0,), (0,)), ((), ())), precision=HI, preferred_element_type=F32)
        gpart[l] = gram.reshape(gpart.shape[1:])

    wire.put(gpart.at[1 - c], gcore, me.at(c=1 - c)).wait_recv()
    a_ref[...] = gpart[c] + gcore[...]
    copies = [
        [wire.put(a_ref.at[h, t], s1.at[h, o - 1], me.along(h, t)) for o, t in me.others(h)] for h in (0, 1)
    ]
    for h in (0, 1):
        arrive(copies[h])
        total = a_ref[h, me.mine(h)]
        for o in range(side - 1):
            total = total + s1[h, o]
        b_ref[h] = total
        copies[h] = [wire.put(b_ref.at[h, t], s2.at[h, o - 1], me.along(1 - h, t)) for o, t in me.others(1 - h)]
    wide = 2 * rank // depth
    tall = b_ref.shape[2] // 2
    tile = lambda t: (slice(t // (depth // 2) * tall, t // (depth // 2) * tall + tall), slice(t % (depth // 2) * wide, t % (depth // 2) * wide + wide))
    for h in (0, 1):
        arrive(copies[h])
        total = b_ref[h, me.mine(1 - h)]
        for o in range(side - 1):
            total = total + s2[h, o]
        for t in range(depth):
            c_ref[t, h] = total[tile(t)]
    arrive([wire.put(c_ref.at[t], s3.at[o - 1], me.at(z=t)) for o, t in me.others_z()])
    total = c_ref[z]
    for o in range(depth - 1):
        total = total + s3[o]
    d_ref[z] = total
    arrive([wire.put(d_ref.at[z], d_ref.at[z], me.at(z=t)) for _, t in me.others_z()])
    for h in (0, 1):
        i, j = me.mine(h), me.mine(1 - h)
        for t in range(depth):
            g_ref[(c, h, i, j) + tile(t)] = d_ref[t, h]
        copies[h] = [
            wire.put(g_ref.at[c, h, i, j], g_ref.at[c, h, i, j], me.along(1 - h, t)) for _, t in me.others(1 - h)
        ]
    for h in (0, 1):
        arrive(copies[h])
        i = me.mine(h)
        copies[h] = [wire.put(g_ref.at[c, h, i], g_ref.at[c, h, i], me.along(h, t)) for _, t in me.others(h)]
    for h in (0, 1):
        arrive(copies[h])
    wire.put(g_ref.at[c], g_ref.at[c], me.at(c=1 - c)).wait_recv()
    wire.finish()


def power(momentum, factor, side, depth):
    layers, rows, width = momentum.shape
    rank = factor.shape[1] * side * side * CORES
    short = rows // depth
    piece = rank // (2 * side * side)
    tile = (depth, 2, piece // 2, 2 * rank // depth)
    steps = layers * (2 * (side - 1) + 1) + layers * (depth - 1)
    steps += 2 + 8 * (side - 1) + 2 * (depth - 1)
    whole = (2, side, side, piece, rank)
    far = max(1, depth // 2)
    p, g = pl.pallas_call(
        functools.partial(power_kernel, layers, side, depth),
        out_shape=(
            jax.ShapeDtypeStruct((layers, short, rank), F32),
            jax.ShapeDtypeStruct((layers,) + whole, F32),
        ),
        in_specs=[pl.BlockSpec(memory_space=pltpu.VMEM)] * 2,
        out_specs=[pl.BlockSpec(memory_space=pltpu.VMEM)] * 2,
        scratch_shapes=[
            pltpu.VMEM((layers, side, side, CORES, factor.shape[1], width), BF16),
            pltpu.VMEM((layers, depth, short, rank), F32),
            pltpu.VMEM((layers, 2, far, short, rank), F32),
            pltpu.VMEM((layers,) + whole, F32),
            pltpu.VMEM(whole, F32),
            pltpu.VMEM(whole, F32),
            pltpu.VMEM((2, side - 1) + whole[2:], F32),
            pltpu.VMEM((2,) + whole[2:], F32),
            pltpu.VMEM((2, side - 1) + whole[3:], F32),
            pltpu.VMEM(tile, F32),
            pltpu.VMEM((depth - 1,) + tile[1:], F32),
            pltpu.VMEM(tile, F32),
            pltpu.SemaphoreType.DMA((steps,)),
            pltpu.SemaphoreType.DMA((steps,)),
        ],
        compiler_params=pltpu.CompilerParams(collective_id=0, has_side_effects=True, vmem_limit_bytes=VMEM_BYTES),
        name="power_gram",
    )(factor, momentum)
    return p, g.reshape(layers, rank, rank)


def right_kernel(layers, side, depth, o_ref, m_ref, all_ref, pair_ref, new_ref, rt, rc, r1, u, r2, sq, sz, send, recv):
    me = Place(side, depth)
    wire = Wire(send, recv)
    x, y, c, z = me.x, me.y, me.c, me.z
    rank = o_ref.shape[-1]
    me.barrier()

    right, left = lax.rem(z + 1, depth), lax.rem(z + depth - 1, depth)
    all_ref[:, z] = o_ref[...]

    def chain_step(l, way, s):
        src = lax.rem(z + depth - (s - 1), depth) if way == 0 else lax.rem(z + s - 1, depth)
        return wire.put(all_ref.at[l, src], all_ref.at[l, src], me.at(z=right if way == 0 else left))

    for l in range(layers):
        pending = {}
        for s in range(1, depth // 2 + 1):
            for way in (0, 1):
                if s <= hops(depth, l)[way]:
                    if s > 1:
                        pending[way].wait_recv()
                    pending[way] = chain_step(l, way, s)
        for way in pending:
            pending[way].wait_recv()
    core = []
    for l in range(layers):
        ortho = all_ref[l].reshape(-1, rank)
        width = m_ref.shape[-1]
        for k in range(width // 256):
            cols = slice(256 * k, 256 * k + 256)
            out = lax.dot_general(ortho, m_ref[l, :, cols], (((0,), (0,)), ((), ())), preferred_element_type=F32)
            rt[l, :, :, :, :, cols] = out.reshape(rt.shape[1:5] + (256,))
        core.append(wire.put(rt.at[l, :, :, 1 - c], rc.at[l], me.at(c=1 - c)))

    copies = []
    for l in range(layers):
        core[l].wait_recv()
        rt[l, :, :, c] += rc[l]
        pick = lambda t: rt.at[l, t, :, c] if l == 0 else rt.at[l, :, t, c]
        copies.append([wire.put(pick(t), r1.at[l, o - 1], me.along(l, t)) for o, t in me.others(l)])
    for l in range(layers):
        arrive(copies[l])
        total = rt[l, x, :, c] if l == 0 else rt[l, :, y, c]
        for o in range(side - 1):
            total = total + r1[l, o]
        u[l] = total
        copies[l] = [wire.put(u.at[l, t], r2.at[l, o - 1], me.along(1 - l, t)) for o, t in me.others(1 - l)]
    sums = []
    for l in range(layers):
        arrive(copies[l])
        total = u[l, me.mine(1 - l)]
        for o in range(side - 1):
            total = total + r2[l, o]
        sums.append(total)
        sq[l] = jnp.broadcast_to(jnp.sum(total * total, axis=1, keepdims=True), sq.shape[1:])
    arrive([wire.put(sq, sz.at[o - 1], me.at(z=t)) for o, t in me.others_z()])
    norm = sq[...]
    for o in range(depth - 1):
        norm = norm + sz[o]
    for l in range(layers):
        normed = (sums[l] * lax.rsqrt(norm[l, :, :1] + 1e-06)).astype(BF16)
        new_ref[l] = normed
        pair_ref[l, 0, x, y, c] = sums[l].astype(BF16)
        pair_ref[l, 1, x, y, c] = normed
        block = pair_ref.at[l, :, x, y, c]
        copies[l] = [wire.put(block, block, me.along(l, t)) for _, t in me.others(l)]
    for l in range(layers):
        arrive(copies[l])
        block = pair_ref.at[l, :, :, y, c] if l == 0 else pair_ref.at[l, :, x, :, c]
        copies[l] = [wire.put(block, block, me.along(1 - l, t)) for _, t in me.others(1 - l)]
    last = []
    for l in range(layers):
        arrive(copies[l])
        block = pair_ref.at[l, :, :, :, c]
        last.append(wire.put(block, block, me.at(c=1 - c)))
    arrive(last)
    wire.finish()


def right_products(ortho, momentum, side, depth):
    layers, rows, width = momentum.shape
    rank = ortho.shape[-1]
    per = rank // (side * side * CORES)
    steps = layers * (depth - 1) + 2 * layers + (depth - 1) + layers * 4 * (side - 1)
    grid = (side, side, CORES, per, width)
    whole, pair, new = pl.pallas_call(
        functools.partial(right_kernel, layers, side, depth),
        out_shape=(
            jax.ShapeDtypeStruct((layers, depth) + ortho.shape[1:], BF16),
            jax.ShapeDtypeStruct((layers, 2) + grid, BF16),
            jax.ShapeDtypeStruct((layers, per, width), BF16),
        ),
        in_specs=[pl.BlockSpec(memory_space=pltpu.VMEM)] * 2,
        out_specs=[pl.BlockSpec(memory_space=pltpu.VMEM)] * 3,
        scratch_shapes=[
            pltpu.VMEM((layers,) + grid, F32),
            pltpu.VMEM((layers, side, side, per, width), F32),
            pltpu.VMEM((layers, side - 1, side, per, width), F32),
            pltpu.VMEM((layers, side, per, width), F32),
            pltpu.VMEM((layers, side - 1, per, width), F32),
            pltpu.VMEM((layers, per, 128), F32),
            pltpu.VMEM((depth - 1, layers, per, 128), F32),
            pltpu.SemaphoreType.DMA((steps,)),
            pltpu.SemaphoreType.DMA((steps,)),
        ],
        compiler_params=pltpu.CompilerParams(collective_id=1, has_side_effects=True, vmem_limit_bytes=VMEM_BYTES),
        name="right_products",
    )(ortho, momentum)
    return whole.reshape(layers, rows, rank), pair.reshape(layers, 2, rank, width), new


def leaf_inverse(x):
    groups = NB // 8
    rows = [x[8 * g : 8 * g + 8, :] for g in range(groups)]
    lane = lax.broadcasted_iota(jnp.int32, (8, NB), 1)
    sub = lax.broadcasted_iota(jnp.int32, (8, NB), 0)
    splat = lambda v, p: jnp.broadcast_to(v[p : p + 1, :], (8, NB))
    out = []
    for g in range(groups):
        base = 8 * g
        inside = (lane >= base) & (lane < base + 8)
        cur = rows[g]
        cols = [jnp.broadcast_to(cur[:, base + q : base + q + 1], (8, NB)) for q in range(8)]
        fwd = jnp.where(inside, jnp.where(lane == sub + base, 1.0, 0.0), cur)
        full = fwd
        pivot = None
        for p in range(8):
            d = splat(cols[p], p)
            m = cols[p] * (1.0 / d)
            mf = jnp.where(sub > p, m, 0.0)
            mj = jnp.where(sub == p, 0.0, m)
            pivot = d if p == 0 else jnp.where(sub == p, d, pivot)
            if p < 7:
                fwd = fwd - mf * splat(fwd, p)
            full = full - mj * splat(full, p)
            for q in range(p + 1, 8):
                cols[q] = cols[q] - mj * splat(cols[q], p)
        out.append(jnp.where(lane < base + 8, fwd * lax.rsqrt(pivot), 0.0))
        if g + 1 < groups:
            full = full / pivot
            parts = [splat(full, q) for q in range(8)]
            for i in range(g + 1, groups):
                r = rows[i]
                acc = jnp.where(inside, 0.0, r)
                for q in range(8):
                    acc = acc - jnp.broadcast_to(r[:, base + q : base + q + 1], (8, NB)) * parts[q]
                rows[i] = acc
    return jnp.concatenate(out, axis=0)

def chol_kernel(layers, n, gram_ref, proj_ref, out_ref, x_ref):
    blocks = n // NB
    x_ref[...] = gram_ref[...]
    colid = lax.broadcasted_iota(jnp.int32, (NB, n), 1) // NB
    ident = (lax.broadcasted_iota(jnp.int32, (NB, n), 1) % NB == lax.broadcasted_iota(jnp.int32, (NB, n), 0)).astype(F32)
    def step(k, carry):
        w = [leaf_inverse(x_ref[l, pl.ds(k * NB, NB), pl.ds(k * NB, NB)]) for l in range(layers)]
        return carry
    for k in range(blocks):
        sl = slice(k * NB, k * NB + NB)
        ws = [leaf_inverse(x_ref[l, sl, sl]) for l in range(layers)]
        for l in range(layers):
            row = jnp.where(colid == k, ident, x_ref[l, sl, :])
            y = jnp.dot(ws[l], row, precision=HI, preferred_element_type=F32)
            x_ref[l, sl, :] = jnp.where(colid <= k, y, 0.0)
            if k + 1 < blocks:
                tail = slice(k * NB + NB, n)
                upd = lax.dot_general(y[:, k * NB + NB :], y, (((0,), (0,)), ((), ())), precision=HI, preferred_element_type=F32)
                keep = x_ref[l, tail, :]
                cid = lax.broadcasted_iota(jnp.int32, keep.shape, 1) // NB
                x_ref[l, tail, :] = jnp.where(cid == k, 0.0, keep) - upd
    for l in range(layers):
        out_ref[l] = lax.dot_general(proj_ref[l], x_ref[l], (((1,), (1,)), ((), ())), precision=HI, preferred_element_type=F32).astype(out_ref.dtype)

def chol_ortho(gram, proj):
    layers, n, _ = gram.shape
    return pl.pallas_call(
        functools.partial(chol_kernel, layers, n),
        out_shape=jax.ShapeDtypeStruct(proj.shape, BF16),
        in_specs=[pl.BlockSpec(memory_space=pltpu.VMEM)] * 2,
        out_specs=pl.BlockSpec(memory_space=pltpu.VMEM),
        scratch_shapes=[pltpu.VMEM((layers, n, n), F32)],
        compiler_params=pltpu.CompilerParams(vmem_limit_bytes=48 * 2**20),
    )(gram, proj)


def solution(mesh):
    side = math.isqrt(mesh.shape["fsdp"] // CORES)
    depth = mesh.shape["tp"]

    def local(momentum, right_factor):
        rank = right_factor.shape[1] * side * side * CORES
        total_rows, total_cols = momentum.shape[1] * side * side * CORES, momentum.shape[2] * depth
        scale = math.sqrt(total_rows * total_cols / rank)
        project, gram = power(momentum, right_factor, side, depth)
        ortho_part = chol_ortho(gram, project)
        ortho, pair, new_factor = right_products(ortho_part, momentum, side, depth)
        feedback = jnp.einsum("lrk,lkd->lrd", ortho, pair[:, 0], preferred_element_type=F32)
        direction = jnp.einsum("lrk,lkd->lrd", ortho, pair[:, 1], preferred_element_type=F32)
        new_momentum = (momentum.astype(F32) - 0.05 * feedback).astype(BF16)
        return new_momentum, (scale * direction).astype(BF16), new_factor

    spec = P(None, "fsdp", "tp")
    return jax.shard_map(local, mesh=mesh, in_specs=(spec, spec), out_specs=(spec, spec, spec), check_vma=False)
```

time: 1020 us -> 256 us (0.25); the launches traced: 1010 us -> 256 us
  waiting for transfers between devices: 616 us -> 0 us
  other arithmetic: 259 us -> 0 us
  Pallas kernels: 0 us -> 241 us
  matrix products: 66.3 us -> 10.1 us
  local copies, waits for them, and re-layouts: 31.9 us -> 3.93 us
  between operations: 19.9 us -> 0.71 us
  blocking collectives: 13.7 us -> 0 us
    all_gather x6 -> x0, waiting for transfers between devices: 286 us -> none  [the longest x2 99.9 us: dion_layers(): lax.all_gather(factor, 'fsdp', axis=1, tiled=True)]
    another operation x35 -> x0, other arithmetic: 245 us -> none  [the longest x30 162 us: invert_gram(): chol = jnp.linalg.cholesky(gram)]
    pallas_call x0 -> x3, Pallas kernels: none -> 241 us  [the longest x1 107 us: power(): pl.pallas_call(functools.partial(power_kernel, layers, side, depth), out_...]
    psum x2 -> x0, waiting for transfers between devices: 215 us -> none  [the longest x1 116 us: dion_layers(): gram = lax.psum(local_gram, 'fsdp')]
    reduce_scatter x2 -> x0, waiting for transfers between devices: 114 us -> none  [dion_layers(): lax.psum_scatter(jnp.einsum('lrk,lrd->kld', ortho, momentum, preferred_el...]
    dot_general x12 -> x2, matrix products: 41.9 us -> 10.1 us  [the longest x1 6.21 us: local(): jnp.einsum('lrk,lkd->lrd', ortho, pair[:, 0], preferred_element_type=F32)]
    another operation x26 -> x0, matrix products: 24.5 us -> none  [the longest x12 15.6 us: invert_gram(): chol = jnp.linalg.cholesky(gram)]
    another operation x35 -> x0, local copies, waits for them, and re-layouts: 22.6 us -> none  [the longest x27 19.5 us: invert_gram(): lax.linalg.triangular_solve(chol, identity, left_side=True, lower=True)]
  transfers between devices with their start and end apart: 10 -> 0, of which waited for: 10 -> 0; matrix products, arithmetic and copies ran while one was open for 8% -> 0% of each run, Pallas kernels for 0% -> 0%
where the time goes in v1:
time: 256 us
  Pallas kernels  241 us (94%)
  matrix products  10.1 us (4%)
  local copies, waits for them, and re-layouts  3.93 us (2%)
    pallas_call x1, Pallas kernels, power(): pl.pallas_call(functools.partial(power_kernel, layers, side, depth), out_...  107 us
    pallas_call x1, Pallas kernels, right_products(): pl.pallas_call(functools.partial(right_kernel, layers, side, depth), out_...  93.4 us
    pallas_call x1, Pallas kernels, chol_ortho(): pl.pallas_call(functools.partial(chol_kernel, layers, n), out_shape=jax.S...  40.1 us
    dot_general x1, matrix products, local(): jnp.einsum('lrk,lkd->lrd', ortho, pair[:, 0], preferred_element_type=F32)  6.21 us

profile of v1, /device:TPU:1, one launch (start us, length us, event | category | flops | bytes accessed | tf_op | source)
XLA Modules:
  0.0 255.7 jit_solution(3460748238706445512)
XLA Ops:
  0.6 0.0 copy-start.3
  0.6 107.4 %power_gram.1 = (f32[2,112,512]{2,1,0:T(8,128)}, f32[2,2,4,4,16,512]{5,4,3,2,1,0:T(8,128)}) custom-call(bf16[2,16,1024]{2,1,0:T(8,128)(2,1)} %q_ref.1, bf16[2,896,1024]{2,1,0:T(8,128)(2,1)} %m_ref.3), custom_call_target="tpu_custom_call" | custom-call | tf_op jit(solution)/shard_map/power_gram/pallas_call | solution.py:210
  108.1 0.0 copy-start
  108.1 1.6 copy-done
  109.7 0.0 copy-start.2
  109.7 1.0 copy-done.2
  110.7 40.1 %shard_map.49.o_ref = bf16[2,112,512]{2,1,0:T(8,128)(2,1)S(1)} custom-call(f32[2,512,512]{2,1,0:T(8,128)S(1)} %bitcast.15, f32[2,112,512]{2,1,0:T(8,128)S(1)} %copy-done.2), custom_call_target="tpu_custom_call" | custom-call | tf_op jit(solution)/shard_map/pallas_call | solution.py:415
  150.8 0.0 copy-start.1
  150.8 0.7 copy-done.1
  151.5 93.4 %right_products.1 = (bf16[2,8,112,512]{3,2,1,0:T(8,128)(2,1)}, bf16[2,2,4,4,2,16,1024]{6,5,4,3,2,1,0:T(8,128)(2,1)}, bf16[2,16,1024]{2,1,0:T(8,128)(2,1)}) custom-call(bf16[2,112,512]{2,1,0:T(8,128)(2,1)} %copy-done.1, bf16[2,896,1024]{2,1,0:T(8,128)(2,1)} %m_ref.3), custom_call_target="tpu_custom_call" | custom-call | tf_op jit(solution)/shard_map/right_products/pallas_call | solution.py:325
  244.9 0.0 copy-done.3
  244.9 0.0 copy-start.5
  244.9 0.0 copy-start.6
  244.9 6.2 %subtract_convert_fusion = bf16[2,896,1024]{2,1,0:T(8,128)(2,1)} fusion(bf16[2,896,1024]{2,1,0:T(8,128)(2,1)S(1)} %copy-done.3, bf16[2,896,512]{2,1,0:T(8,128)(2,1)} %bitcast.18, bf16[2,2,512,1024]{3,2,1,0:T(8,128)(2,1)} %bitcast.16), kind=kOutput, calls=%fused_computation.1 | convolution fusion | flops 1886388224 | bytes 11272192 | tf_op jit(solution)/shard_map/lrk,lkd->lrd/dot_general | solution.py:436
  251.1 0.0 copy-done.5
  251.1 0.0 copy-done.6
  251.1 0.0 copy-start.4
  251.1 3.9 %multiply_convert_fusion = bf16[2,896,1024]{2,1,0:T(8,128)(2,1)} fusion(bf16[2,896,512]{2,1,0:T(8,128)(2,1)S(1)} %bitcast.19, bf16[2,2,512,1024]{3,2,1,0:T(8,128)(2,1)S(1)} %bitcast.17), kind=kOutput, calls=%fused_computation | convolution fusion | flops 1882718208 | bytes 7602176 | tf_op jit(solution)/shard_map/lrk,lkd->lrd/dot_general | solution.py:437
  255.0 0.0 copy-done.4
  255.0 0.6 copy.10
Async XLA Ops:
  0.6 244.3 %copy-start.3 = (bf16[2,896,1024]{2,1,0:T(8,128)(2,1)S(1)}, bf16[2,896,1024]{2,1,0:T(8,128)(2,1)}, u32[]{:S(2)}) copy-start(bf16[2,896,1024]{2,1,0:T(8,128)(2,1)} %m_ref.3) | copy-start | bytes 11010052
  108.1 1.6 copy-start
  109.7 1.0 copy-start.2
  150.8 0.7 copy-start.1
  244.9 6.2 %copy-start.5 = (bf16[2,2,4,4,2,16,1024]{6,5,4,3,2,1,0:T(8,128)(2,1)S(1)}, bf16[2,2,4,4,2,16,1024]{6,5,4,3,2,1,0:T(8,128)(2,1)}, u32[]{:S(2)}) copy-start(bf16[2,2,4,4,2,16,1024]{6,5,4,3,2,1,0:T(8,128)(2,1)} %get-tuple-element.11) | copy-start | bytes 12582916
  244.9 6.2 %copy-start.6 = (bf16[2,8,112,512]{3,2,1,0:T(8,128)(2,1)S(1)}, bf16[2,8,112,512]{3,2,1,0:T(8,128)(2,1)}, u32[]{:S(2)}) copy-start(bf16[2,8,112,512]{3,2,1,0:T(8,128)(2,1)} %get-tuple-element.10) | copy-start | bytes 5505028
  251.1 3.9 %copy-start.4 = (bf16[2,16,1024]{2,1,0:T(8,128)(2,1)S(1)}, bf16[2,16,1024]{2,1,0:T(8,128)(2,1)}, u32[]{:S(2)}) copy-start(bf16[2,16,1024]{2,1,0:T(8,128)(2,1)} %get-tuple-element.18) | copy-start | bytes 196612

commit v2 on v1

v2 whole, which is shorter than its diff:
```python
import functools
import math

import jax
import jax.numpy as jnp
from jax import lax
from jax.experimental import pallas as pl
from jax.experimental.pallas import tpu as pltpu
from jax.sharding import PartitionSpec as P

MESH = pl.DeviceIdType.MESH
HI = lax.Precision.HIGHEST
CORES = 2
NB = 128
VMEM_BYTES = 36 * 2**20
F32 = jnp.float32
BF16 = jnp.bfloat16


class Place:
    def __init__(self, side, depth):
        f, self.z = lax.axis_index("fsdp"), lax.axis_index("tp")
        self.side, self.depth = side, depth
        self.x, self.y, self.c = f // (side * CORES), (f // CORES) % side, f % CORES

    def at(self, x=None, y=None, c=None, z=None):
        x = self.x if x is None else x
        y = self.y if y is None else y
        c = self.c if c is None else c
        z = self.z if z is None else z
        return ((x * self.side + y) * CORES + c, z)

    def along(self, axis, t):
        return self.at(x=t) if axis == 0 else self.at(y=t)

    def mine(self, axis):
        return self.x if axis == 0 else self.y

    def others(self, axis):
        return [(o, lax.rem(self.mine(axis) + o, self.side)) for o in range(1, self.side)]

    def others_z(self):
        return [(o, lax.rem(self.z + o, self.depth)) for o in range(1, self.depth)]

    def barrier(self):
        sem = pltpu.get_barrier_semaphore()
        devices = [self.at(c=1 - self.c)]
        devices += [self.along(a, t) for a in (0, 1) for _, t in self.others(a)]
        devices += [self.at(z=t) for _, t in self.others_z()]
        for device in devices:
            pl.semaphore_signal(sem, inc=1, device_id=device, device_id_type=MESH)
        pl.semaphore_wait(sem, len(devices))


class Wire:
    def __init__(self, send, recv):
        self.send, self.recv, self.used, self.copies = send, recv, 0, []

    def put(self, src, dst, device):
        n = self.used
        self.used += 1
        copy = pltpu.make_async_remote_copy(
            src_ref=src,
            dst_ref=dst,
            send_sem=self.send.at[n],
            recv_sem=self.recv.at[n],
            device_id=device,
            device_id_type=MESH,
        )
        copy.start()
        self.copies.append(copy)
        return copy

    def finish(self):
        for copy in self.copies:
            copy.wait_send()


def halves(ref):
    wide = ref.shape[-1] // 2
    lead = (slice(None),) * (len(ref.shape) - 1)
    return ref.at[lead + (slice(0, wide),)], ref.at[lead + (slice(wide, 2 * wide),)]


def gather_ring(me, wire, axis, pick):
    t, n = me.mine(axis), me.side
    after, before = lax.rem(t + 1, n), lax.rem(t + n - 1, n)
    if n == 2:
        copies = [wire.put(pick(t), pick(t), me.along(axis, after))]
    else:
        up = wire.put(pick(t), pick(t), me.along(axis, after))
        down = wire.put(pick(t), pick(t), me.along(axis, before))
        yield
        up.wait_recv()
        block = halves(pick(before))[0]
        copies = [wire.put(block, block, me.along(axis, after))]
        down.wait_recv()
        block = halves(pick(after))[1]
        copies.append(wire.put(block, block, me.along(axis, before)))
    yield
    arrive(copies)


def reduce_ring(me, wire, axis, pick, far, near, out):
    t, n = me.mine(axis), me.side
    after, before = lax.rem(t + 1, n), lax.rem(t + n - 1, n)
    if n == 2:
        copies = [wire.put(pick(after), near.at[0], me.along(axis, after))]
    else:
        up, down = me.along(axis, after), me.along(axis, before)
        cross = halves(pick(lax.rem(t + 2, n)))
        to_up, to_down = halves(pick(after)), halves(pick(before))
        at_up, at_down = halves(near.at[0]), halves(near.at[1])
        first = [wire.put(cross[0], far.at[0], up), wire.put(cross[1], far.at[1], down)]
        copies = [wire.put(to_up[1], at_up[1], up), wire.put(to_down[0], at_down[0], down)]
        yield
        first[0].wait_recv()
        to_up[0][...] += far[0]
        copies.append(wire.put(to_up[0], at_up[0], up))
        first[1].wait_recv()
        to_down[1][...] += far[1]
        copies.append(wire.put(to_down[1], at_down[1], down))
    yield
    arrive(copies)
    out[...] = pick(t)[...] + near[0] if n == 2 else pick(t)[...] + near[0] + near[1]


def gather_direct(me, wire, axis, pick):
    mine = pick(me.mine(axis))
    copies = [wire.put(mine, mine, me.along(axis, t)) for _, t in me.others(axis)]
    yield
    arrive(copies)


def reduce_direct(me, wire, axis, pick, near, out):
    copies = [wire.put(pick(t), near.at[o - 1], me.along(axis, t)) for o, t in me.others(axis)]
    yield
    arrive(copies)
    total = pick(me.mine(axis))[...]
    for o in range(me.side - 1):
        total = total + near[o]
    out[...] = total


def together(*parts):
    parts = list(parts)
    while parts:
        for part in list(parts):
            if next(part, parts) is parts:
                parts.remove(part)


def arrive(copies):
    for copy in copies:
        copy.wait_recv()


def hops(depth, layer):
    far, near = depth // 2, depth - 1 - depth // 2
    return (far, near) if layer % 2 == 0 else (near, far)


def staged(parts):
    while parts:
        for part in list(parts):
            if next(part, parts) is parts:
                parts.remove(part)
        if parts:
            yield


def place_block(ref, n, block):
    piece = ref.shape[-2]
    flat, side = n * NB, ref.shape[1]
    done = 0
    while done < NB:
        index, offset = (flat + done) // piece, (flat + done) % piece
        rows = min(piece - offset, NB - done)
        ref[index // (side * side), index // side % side, index % side, offset : offset + rows] = block[done : done + rows]
        done += rows


def power_kernel(layers, side, depth, q_ref, m_hbm, p_ref, g_ref, m_ref, qall, part, chain, pcore, a_ref, near1, b_ref, near2, t_ref, s3, send, recv, load):
    me = Place(side, depth)
    wire = Wire(send, recv)
    x, y, c, z = me.x, me.y, me.c, me.z
    rank = p_ref.shape[-1]
    loads = [pltpu.make_async_copy(m_hbm.at[l], m_ref.at[l], load.at[l]) for l in range(layers)]
    for copy in loads:
        copy.start()
    qall[:, x, y, c] = q_ref[...]
    me.barrier()

    def factor_rows(l):
        yield from gather_direct(me, wire, l, lambda t: qall.at[l, t, y, c] if l == 0 else qall.at[l, x, t, c])
        yield from gather_direct(me, wire, 1 - l, lambda t: qall.at[l, :, t, c] if l == 0 else qall.at[l, t, :, c])
        crossing.append(wire.put(qall.at[l, :, :, c], qall.at[l, :, :, c], me.at(c=1 - c)))

    crossing = []
    together(*[factor_rows(l) for l in range(layers)])

    right, left = lax.rem(z + 1, depth), lax.rem(z + depth - 1, depth)
    rows = part.shape[2]

    def chain_step(l, way, s):
        count = hops(depth, l)[way]
        ahead = count - s + 1
        dest = lax.rem(z + ahead, depth) if way == 0 else lax.rem(z + depth - ahead, depth)
        src = part.at[l, dest]
        if s > 1:
            src = chain.at[l, way, s - 2]
            src[...] += part[l, dest]
        return wire.put(src, chain.at[l, way, s - 1], me.at(z=right if way == 0 else left))

    pending = {}
    for l in range(layers):
        crossing[l].wait_recv()
        loads[l].wait()
        factor = qall[l].reshape(rank, -1)

        @pl.loop(0, depth // 2)
        def _(i):
            lhs = m_ref[l, pl.ds(pl.multiple_of(i * 2 * rows, 16), 2 * rows), :]
            out = lax.dot_general(lhs, factor, (((1,), (1,)), ((), ())), preferred_element_type=F32)
            part[l, pl.ds(2 * i, 2)] = out.reshape(2, rows, rank)

        for way in (0, 1):
            if hops(depth, l)[way]:
                pending[l, way] = chain_step(l, way, 1)
    for s in range(2, depth // 2 + 1):
        for l in range(layers):
            for way in (0, 1):
                if s <= hops(depth, l)[way]:
                    pending[l, way].wait_recv()
                    pending[l, way] = chain_step(l, way, s)
    for l in range(layers):
        total = part[l, z]
        for way in (0, 1):
            count = hops(depth, l)[way]
            if count:
                pending[l, way].wait_recv()
                total = total + chain[l, way, count - 1]
        p_ref[l, z] = total

    def gather_project(l):
        pending = {}
        for s in range(1, depth // 2 + 1):
            for way in (0, 1):
                if s <= hops(depth, l)[way]:
                    if s > 1:
                        pending[way].wait_recv()
                    src = lax.rem(z + depth - (s - 1), depth) if way == 0 else lax.rem(z + s - 1, depth)
                    block = p_ref.at[l, src]
                    pending[way] = wire.put(block, block, me.at(z=right if way == 0 else left))
            yield
        arrive(list(pending.values()))

    def sum_gram():
        swap = wire.put(p_ref.at[1 - c, z], pcore, me.at(c=1 - c))
        yield
        swap.wait_recv()
        both = jnp.concatenate([p_ref[c, z], pcore[...]], axis=0)
        blocks = rank // NB
        n = 0
        for i in range(blocks):
            gram = lax.dot_general(both[:, i * NB : i * NB + NB], both[:, i * NB :], (((0,), (0,)), ((), ())), precision=HI, preferred_element_type=F32)
            for j in range(blocks - i):
                place_block(a_ref, n, gram[:, j * NB : j * NB + NB])
                n += 1
        planes = [sum_plane(0), sum_plane(1)]
        yield from staged(planes)
        copies = [wire.put(t_ref, s3.at[o - 1], me.at(z=t)) for o, t in me.others_z()]
        yield
        arrive(copies)
        total = t_ref[...]
        for o in range(depth - 1):
            total = total + s3[o]
        for h in (0, 1):
            g_ref[h, me.mine(h), me.mine(1 - h)] = total[h]
        yield from staged([spread_plane(0), spread_plane(1)])

    def sum_plane(h):
        yield from reduce_direct(me, wire, h, lambda t: a_ref.at[h, t], near1.at[h], b_ref.at[h])
        yield from reduce_direct(me, wire, 1 - h, lambda t: b_ref.at[h, t], near2.at[h], t_ref.at[h])

    def spread_plane(h):
        i = me.mine(h)
        yield from gather_direct(me, wire, 1 - h, lambda t: g_ref.at[h, i, t])
        yield from gather_direct(me, wire, h, lambda t: g_ref.at[h, t])

    together(sum_gram(), *[gather_project(l) for l in range(layers)])
    wire.finish()


def power(momentum, factor, side, depth):
    layers, rows, width = momentum.shape
    rank = factor.shape[1] * side * side * CORES
    short = rows // depth
    blocks = rank // NB
    piece = blocks * (blocks + 1) // 2 * NB // (2 * side * side)
    whole = (2, side, side, piece, NB)
    p, g = pl.pallas_call(
        functools.partial(power_kernel, layers, side, depth),
        out_shape=(
            jax.ShapeDtypeStruct((layers, depth, short, rank), F32),
            jax.ShapeDtypeStruct(whole, F32),
        ),
        in_specs=[pl.BlockSpec(memory_space=pltpu.VMEM), pl.BlockSpec(memory_space=pl.ANY)],
        out_specs=[pl.BlockSpec(memory_space=pltpu.VMEM)] * 2,
        scratch_shapes=[
            pltpu.VMEM(momentum.shape, BF16),
            pltpu.VMEM((layers, side, side, CORES, factor.shape[1], width), BF16),
            pltpu.VMEM((layers, depth, short, rank), F32),
            pltpu.VMEM((layers, 2, max(1, depth // 2), short, rank), F32),
            pltpu.VMEM((short, rank), F32),
            pltpu.VMEM(whole, F32),
            pltpu.VMEM((2, side - 1) + whole[2:], F32),
            pltpu.VMEM((2,) + whole[2:], F32),
            pltpu.VMEM((2, side - 1) + whole[3:], F32),
            pltpu.VMEM((2,) + whole[3:], F32),
            pltpu.VMEM((depth - 1, 2) + whole[3:], F32),
            pltpu.SemaphoreType.DMA((100,)),
            pltpu.SemaphoreType.DMA((100,)),
            pltpu.SemaphoreType.DMA((layers,)),
        ],
        compiler_params=pltpu.CompilerParams(collective_id=0, has_side_effects=True, vmem_limit_bytes=VMEM_BYTES),
        name="power_gram",
    )(factor, momentum)
    return p, g.reshape(-1, NB, NB)


def right_kernel(layers, side, depth, w_ref, p_hbm, m_hbm, all_ref, rb_ref, s_ref, new_ref, m_ref, p_ref, wall, rt, rc, far1, near1, u, far2, near2, tot, sq, sz, send, recv, load):
    me = Place(side, depth)
    wire = Wire(send, recv)
    x, y, c, z = me.x, me.y, me.c, me.z
    rank = w_ref.shape[-1]
    loads = [pltpu.make_async_copy(m_hbm.at[l], m_ref.at[l], load.at[l]) for l in range(layers)]
    ploads = [pltpu.make_async_copy(p_hbm.at[l], p_ref.at[l], load.at[layers + l]) for l in range(layers)]
    for copy in ploads + loads:
        copy.start()
    wall[c] = w_ref[...]
    me.barrier()

    wire.put(wall.at[c], wall.at[c], me.at(c=1 - c)).wait_recv()
    core = []
    for l in range(layers):
        ploads[l].wait()

        @pl.loop(0, depth // 2)
        def _(i):
            lhs = p_ref[l, pl.ds(2 * i, 2)].reshape(-1, rank)
            out = lax.dot_general(lhs, wall[l], (((1,), (1,)), ((), ())), precision=HI, preferred_element_type=F32)
            all_ref[l, pl.ds(2 * i, 2)] = out.astype(BF16).reshape(2, -1, rank)

        loads[l].wait()
        ortho = all_ref[l].reshape(-1, rank)
        width = m_ref.shape[-1]
        for k in range(width // 256):
            cols = slice(256 * k, 256 * k + 256)
            out = lax.dot_general(ortho, m_ref[l, :, cols], (((0,), (0,)), ((), ())), preferred_element_type=F32)
            rt[l, :, :, :, :, cols] = out.reshape(rt.shape[1:5] + (256,))
        core.append(wire.put(rt.at[l, :, :, 1 - c], rc.at[l], me.at(c=1 - c)))

    def sum_rows(l):
        core[l].wait_recv()
        rc[l] += rt[l, :, :, c]
        pick = lambda t: rc.at[l, t] if l == 0 else rc.at[l, :, t]
        yield from reduce_ring(me, wire, l, pick, far1.at[l], near1.at[l], u.at[l])
        yield from reduce_ring(me, wire, 1 - l, lambda t: u.at[l, t], far2.at[l], near2.at[l], tot.at[l])

    together(*[sum_rows(l) for l in range(layers)])

    def gather_rows(l):
        rb_ref[l, x, y, c] = tot[l].astype(BF16)
        yield from gather_ring(me, wire, l, lambda t: rb_ref.at[l, t, y, c] if l == 0 else rb_ref.at[l, x, t, c])
        yield from gather_ring(me, wire, 1 - l, lambda t: rb_ref.at[l, :, t, c] if l == 0 else rb_ref.at[l, t, :, c])
        cross = wire.put(rb_ref.at[l, :, :, c], rb_ref.at[l, :, :, c], me.at(c=1 - c))
        yield
        yield
        cross.wait_recv()

    def gather_norms():
        for l in range(layers):
            sq[l] = jnp.broadcast_to(jnp.sum(tot[l] * tot[l], axis=1, keepdims=True), sq.shape[1:])
        copies = [wire.put(sq, sz.at[o - 1], me.at(z=t)) for o, t in me.others_z()]
        yield
        arrive(copies)
        norm = sq[...]
        for o in range(depth - 1):
            norm = norm + sz[o]
        factor = lax.rsqrt(norm + 1e-06)
        for l in range(layers):
            s_ref[l, x, y, c] = factor[l]
            new_ref[l] = (tot[l] * factor[l, :, :1]).astype(BF16)
        mine = s_ref.at[:, x, y, c]
        copies = [wire.put(mine, mine, me.along(0, t)) for _, t in me.others(0)]
        yield
        arrive(copies)
        mine = s_ref.at[:, :, y, c]
        copies = [wire.put(mine, mine, me.along(1, t)) for _, t in me.others(1)]
        yield
        arrive(copies)
        copies = [wire.put(s_ref.at[:, :, :, c], s_ref.at[:, :, :, c], me.at(c=1 - c))]
        yield
        arrive(copies)

    together(*[gather_rows(l) for l in range(layers)], gather_norms())
    wire.finish()


def right_products(inverse, project, momentum, side, depth):
    layers, rows, width = momentum.shape
    rank = project.shape[-1]
    per = rank // (side * side * CORES)
    grid = (side, side, CORES, per)
    whole, rb, s, new = pl.pallas_call(
        functools.partial(right_kernel, layers, side, depth),
        out_shape=(
            jax.ShapeDtypeStruct(project.shape, BF16),
            jax.ShapeDtypeStruct((layers,) + grid + (width,), BF16),
            jax.ShapeDtypeStruct((layers,) + grid + (128,), F32),
            jax.ShapeDtypeStruct((layers, per, width), BF16),
        ),
        in_specs=[pl.BlockSpec(memory_space=pltpu.VMEM)] + [pl.BlockSpec(memory_space=pl.ANY)] * 2,
        out_specs=[pl.BlockSpec(memory_space=pltpu.VMEM)] * 4,
        scratch_shapes=[
            pltpu.VMEM(momentum.shape, BF16),
            pltpu.VMEM(project.shape, F32),
            pltpu.VMEM((layers, rank, rank), F32),
            pltpu.VMEM((layers,) + grid + (width,), F32),
            pltpu.VMEM((layers, side, side, per, width), F32),
            pltpu.VMEM((layers, 2, side, per, width // 2), F32),
            pltpu.VMEM((layers, 2, side, per, width), F32),
            pltpu.VMEM((layers, side, per, width), F32),
            pltpu.VMEM((layers, 2, per, width // 2), F32),
            pltpu.VMEM((layers, 2, per, width), F32),
            pltpu.VMEM((layers, per, width), F32),
            pltpu.VMEM((layers, per, 128), F32),
            pltpu.VMEM((depth - 1, layers, per, 128), F32),
            pltpu.SemaphoreType.DMA((100,)),
            pltpu.SemaphoreType.DMA((100,)),
            pltpu.SemaphoreType.DMA((2 * layers,)),
        ],
        compiler_params=pltpu.CompilerParams(collective_id=1, has_side_effects=True, vmem_limit_bytes=VMEM_BYTES),
        name="right_products",
    )(inverse, project, momentum)
    return whole.reshape(layers, rows, rank), rb.reshape(layers, rank, width), s.reshape(layers, rank, 128), new


def final_kernel(scale, o_ref, m_ref, rb_ref, s_ref, mom_ref, up_ref):
    ortho, rb = o_ref[0], rb_ref[0]
    feedback = jnp.dot(ortho, rb, preferred_element_type=F32)
    mom_ref[0] = (m_ref[0].astype(F32) - 0.05 * feedback).astype(BF16)
    normed = (rb.astype(F32) * s_ref[0, :, :1]).astype(BF16)
    up_ref[0] = (scale * jnp.dot(ortho, normed, preferred_element_type=F32)).astype(BF16)


def final_products(ortho, momentum, rb, s, scale):
    layers, rows, rank = ortho.shape
    width = momentum.shape[-1]
    block = min(width, 256)
    cols = lambda n: pl.BlockSpec((1, n, block), lambda l, i: (l, 0, i))
    full = lambda n, w: pl.BlockSpec((1, n, w), lambda l, i: (l, 0, 0))
    return pl.pallas_call(
        functools.partial(final_kernel, scale),
        grid=(layers, width // block),
        out_shape=[jax.ShapeDtypeStruct(momentum.shape, BF16)] * 2,
        in_specs=[full(rows, rank), cols(rows), cols(rank), full(rank, 128)],
        out_specs=[cols(rows)] * 2,
        compiler_params=pltpu.CompilerParams(vmem_limit_bytes=VMEM_BYTES),
        name="final_products",
    )(ortho, momentum, rb, s)


def leaf_inverse(x):
    groups = NB // 8
    rows = [x[8 * g : 8 * g + 8, :] for g in range(groups)]
    lane = lax.broadcasted_iota(jnp.int32, (8, NB), 1)
    sub = lax.broadcasted_iota(jnp.int32, (8, NB), 0)
    splat = lambda v, p: jnp.broadcast_to(v[p : p + 1, :], (8, NB))
    out = []
    for g in range(groups):
        base = 8 * g
        inside = (lane >= base) & (lane < base + 8)
        cur = rows[g]
        cols = [jnp.broadcast_to(cur[:, base + q : base + q + 1], (8, NB)) for q in range(8)]
        fwd = jnp.where(inside, jnp.where(lane == sub + base, 1.0, 0.0), cur)
        full = fwd
        pivot = None
        for p in range(8):
            d = splat(cols[p], p)
            inv = pl.reciprocal(d, approx=True)
            inv = inv * (2.0 - d * inv)
            m = cols[p] * inv
            mf = jnp.where(sub > p, m, 0.0)
            mj = jnp.where(sub == p, 0.0, m)
            pivot = d if p == 0 else jnp.where(sub == p, d, pivot)
            ipivot = inv if p == 0 else jnp.where(sub == p, inv, ipivot)
            if p < 7:
                fwd = fwd - mf * splat(fwd, p)
            full = full - mj * splat(full, p)
            for q in range(p + 1, 8):
                cols[q] = cols[q] - mj * splat(cols[q], p)
        out.append(jnp.where(lane < base + 8, fwd * lax.rsqrt(pivot), 0.0))
        if g + 1 < groups:
            full = full * ipivot
            parts = [splat(full, q) for q in range(8)]
            for i in range(g + 1, groups):
                r = rows[i]
                acc = jnp.where(inside, 0.0, r)
                for q in range(8):
                    acc = acc - jnp.broadcast_to(r[:, base + q : base + q + 1], (8, NB)) * parts[q]
                rows[i] = acc
    return jnp.concatenate(out, axis=0)

def chol_kernel(n, gram_ref, x_ref):
    blocks = n // NB
    x_ref[...] = jnp.zeros_like(x_ref)
    b = 0
    for i in range(blocks):
        for j in range(i, blocks):
            x_ref[i * NB : i * NB + NB, j * NB : j * NB + NB] = gram_ref[b]
            b += 1
    colid = lax.broadcasted_iota(jnp.int32, (NB, n), 1) // NB
    ident = (lax.broadcasted_iota(jnp.int32, (NB, n), 1) % NB == lax.broadcasted_iota(jnp.int32, (NB, n), 0)).astype(F32)
    for k in range(blocks):
        sl = slice(k * NB, k * NB + NB)
        w = leaf_inverse(x_ref[sl, sl])
        row = jnp.where(colid == k, ident, x_ref[sl, :])
        out = jnp.dot(w, row, precision=HI, preferred_element_type=F32)
        x_ref[sl, :] = jnp.where(colid <= k, out, 0.0)
        if k + 1 < blocks:
            tail = slice(k * NB + NB, n)
            upd = lax.dot_general(out[:, k * NB + NB :], out, (((0,), (0,)), ((), ())), precision=HI, preferred_element_type=F32)
            keep = x_ref[tail, :]
            cid = lax.broadcasted_iota(jnp.int32, keep.shape, 1) // NB
            x_ref[tail, :] = jnp.where(cid == k, 0.0, keep) - upd


def chol_inverse(gram):
    n = NB * (math.isqrt(8 * gram.shape[0] + 1) // 2)
    return pl.pallas_call(
        functools.partial(chol_kernel, n),
        out_shape=jax.ShapeDtypeStruct((n, n), F32),
        in_specs=[pl.BlockSpec(memory_space=pltpu.VMEM)],
        out_specs=pl.BlockSpec(memory_space=pltpu.VMEM),
        compiler_params=pltpu.CompilerParams(vmem_limit_bytes=VMEM_BYTES),
        name="chol_inverse",
    )(gram)


def solution(mesh):
    side = math.isqrt(mesh.shape["fsdp"] // CORES)
    depth = mesh.shape["tp"]

    def local(momentum, right_factor):
        rank = right_factor.shape[1] * side * side * CORES
        total_rows, total_cols = momentum.shape[1] * side * side * CORES, momentum.shape[2] * depth
        scale = math.sqrt(total_rows * total_cols / rank)
        project, gram = power(momentum, right_factor, side, depth)
        inverse = chol_inverse(gram)
        ortho, rb, s, new_factor = right_products(inverse, project, momentum, side, depth)
        new_momentum, update = final_products(ortho, momentum, rb, s, scale)
        return new_momentum, update, new_factor

    spec = P(None, "fsdp", "tp")
    return jax.shard_map(local, mesh=mesh, in_specs=(spec, spec), out_specs=(spec, spec, spec), check_vma=False)
```

time: 256 us -> 208 us (0.81)
  Pallas kernels: 241 us -> 204 us
  matrix products: 10.1 us -> 0 us
    pallas_call x1, Pallas kernels: 93.4 us -> 57.7 us  [right_products(): pl.pallas_call(functools.partial(right_kernel, layers, side, depth), out_...]
    dot_general x2 -> x0, matrix products: 10.1 us -> none  [the longest x1 6.21 us: local(): jnp.einsum('lrk,lkd->lrd', ortho, pair[:, 0], preferred_element_type=F32)]
    pallas_call x1 -> x2, Pallas kernels: 40.1 us -> 32.6 us  [the longest x1 25.1 us: chol_inverse(): pl.pallas_call(functools.partial(chol_kernel, n), out_shape=jax.ShapeDtyp...]
    pallas_call x1, Pallas kernels: 107 us -> 114 us  [power(): pl.pallas_call(functools.partial(power_kernel, layers, side, depth), out_...]
where the time goes in v2:
time: 208 us
  Pallas kernels  204 us (98%)
  local copies, waits for them, and re-layouts  3.5 us (2%)
    pallas_call x1, Pallas kernels, power(): pl.pallas_call(functools.partial(power_kernel, layers, side, depth), out_...  114 us
    pallas_call x1, Pallas kernels, right_products(): pl.pallas_call(functools.partial(right_kernel, layers, side, depth), out_...  57.7 us
    pallas_call x1, Pallas kernels, chol_inverse(): pl.pallas_call(functools.partial(chol_kernel, n), out_shape=jax.ShapeDtyp...  25.1 us
    pallas_call x1, Pallas kernels, final_products(): pl.pallas_call(functools.partial(final_kernel, scale), grid=(layers, widt...  7.43 us

profile of v2, /device:TPU:1, one launch (start us, length us, event | category | flops | bytes accessed | tf_op | source)
XLA Modules:
  0.0 208.1 jit_solution(11743548571553748224)
XLA Ops:
  0.6 0.0 copy-start
  0.6 2.0 copy-done
  2.7 0.0 copy-start.2
  2.7 0.8 copy-done.2
  3.5 0.0 copy-start.1
  3.5 113.7 %power_gram.1 = (f32[2,8,112,512]{3,2,1,0:T(8,128)S(1)}, f32[2,4,4,40,128]{4,3,2,1,0:T(8,128)S(1)}) custom-call(bf16[2,16,1024]{2,1,0:T(8,128)(2,1)S(1)} %copy-done.2, bf16[2,896,1024]{2,1,0:T(8,128)(2,1)S(1)} %copy-done), custom_call_target="tpu_custom_call" | custom-call | tf_op jit(solution)/shard_map/power_gram/pallas_call | solution.py:302
  117.2 25.1 %chol_inverse.1.w_ref = f32[512,512]{1,0:T(8,128)S(1)} custom-call(f32[10,128,128]{2,1,0:T(8,128)S(1)} %bitcast.6), custom_call_target="tpu_custom_call" | custom-call | tf_op jit(solution)/shard_map/chol_inverse/pallas_call | solution.py:542
  142.4 0.0 copy-done.1
  142.4 57.7 %right_products.1 = (bf16[2,8,112,512]{3,2,1,0:T(8,128)(2,1)S(1)}, bf16[2,4,4,2,16,1024]{5,4,3,2,1,0:T(8,128)(2,1)S(1)}, f32[2,4,4,2,16,128]{5,4,3,2,1,0:T(8,128)S(1)}, bf16[2,16,1024]{2,1,0:T(8,128)(2,1)S(1)}) custom-call(f32[512,512]{1,0:T(8,128)S(1)} %chol_inverse.1.w_ref, f32[2,8,112,512]{3,2,1,0:T(8,128)S(1)} %get-tuple-element.12.p_hbm, ...), custom_call_target="tpu_custom_call" | custom-call | tf_op jit(solution)/shard_map/right_products/pallas_call | solution.py:416
  200.1 7.4 %final_products.1 = (bf16[2,896,1024]{2,1,0:T(8,128)(2,1)}, bf16[2,896,1024]{2,1,0:T(8,128)(2,1)}) custom-call(bf16[2,896,512]{2,1,0:T(8,128)(2,1)S(1)} %bitcast.5, bf16[2,896,1024]{2,1,0:T(8,128)(2,1)S(1)} %copy-done.1, bf16[2,512,1024]{2,1,0:T(8,128)(2,1)S(1)} %bitcast.4, f32[2,512,128]{2,1,0:T(8,128)S(1)} %bitcast.7), custom_call_target="tpu_custom_call" | custom-call | tf_op jit(solution)/shard_map/final_products/pallas_call | solution.py:464
  207.5 0.6 copy.6
Async XLA Ops:
  0.6 2.0 copy-start
  2.7 0.8 copy-start.2
  3.5 138.9 %copy-start.1 = (bf16[2,896,1024]{2,1,0:T(8,128)(2,1)S(1)}, bf16[2,896,1024]{2,1,0:T(8,128)(2,1)}, u32[]{:S(2)}) copy-start(bf16[2,896,1024]{2,1,0:T(8,128)(2,1)} %m_ref.1) | copy-start | bytes 11010052

commit v3 on v2

v3 whole, which is shorter than its diff:
```python
import functools
import math

import jax
import jax.numpy as jnp
from jax import lax
from jax.experimental import pallas as pl
from jax.experimental.pallas import tpu as pltpu
from jax.sharding import PartitionSpec as P

MESH = pl.DeviceIdType.MESH
HI = lax.Precision.HIGHEST
CORES = 2
NB = 128
VMEM_BYTES = 48 * 2**20
F32 = jnp.float32
BF16 = jnp.bfloat16


class Place:
    def __init__(self, side, depth):
        f, self.z = lax.axis_index("fsdp"), lax.axis_index("tp")
        self.side, self.depth = side, depth
        self.x, self.y, self.c = f // (side * CORES), (f // CORES) % side, f % CORES

    def at(self, x=None, y=None, c=None, z=None):
        x = self.x if x is None else x
        y = self.y if y is None else y
        c = self.c if c is None else c
        z = self.z if z is None else z
        return ((x * self.side + y) * CORES + c, z)

    def along(self, axis, t):
        return self.at(x=t) if axis == 0 else self.at(y=t)

    def mine(self, axis):
        return self.x if axis == 0 else self.y

    def others(self, axis):
        return [(o, lax.rem(self.mine(axis) + o, self.side)) for o in range(1, self.side)]

    def others_z(self):
        return [(o, lax.rem(self.z + o, self.depth)) for o in range(1, self.depth)]

    def barrier(self):
        sem = pltpu.get_barrier_semaphore()
        devices = [self.at(c=1 - self.c)]
        devices += [self.along(a, t) for a in (0, 1) for _, t in self.others(a)]
        devices += [self.at(z=t) for _, t in self.others_z()]
        for device in devices:
            pl.semaphore_signal(sem, inc=1, device_id=device, device_id_type=MESH)
        pl.semaphore_wait(sem, len(devices))


class Wire:
    def __init__(self, send, recv):
        self.send, self.recv, self.used, self.copies = send, recv, 0, []

    def put(self, src, dst, device):
        n = self.used
        self.used += 1
        copy = pltpu.make_async_remote_copy(
            src_ref=src,
            dst_ref=dst,
            send_sem=self.send.at[n],
            recv_sem=self.recv.at[n],
            device_id=device,
            device_id_type=MESH,
        )
        copy.start()
        self.copies.append(copy)
        return copy

    def finish(self):
        for copy in self.copies:
            copy.wait_send()


def halves(ref):
    wide = ref.shape[-1] // 2
    lead = (slice(None),) * (len(ref.shape) - 1)
    return ref.at[lead + (slice(0, wide),)], ref.at[lead + (slice(wide, 2 * wide),)]


def gather_ring(me, wire, axis, pick):
    t, n = me.mine(axis), me.side
    after, before = lax.rem(t + 1, n), lax.rem(t + n - 1, n)
    if n == 2:
        copies = [wire.put(pick(t), pick(t), me.along(axis, after))]
    else:
        up = wire.put(pick(t), pick(t), me.along(axis, after))
        down = wire.put(pick(t), pick(t), me.along(axis, before))
        yield
        up.wait_recv()
        block = halves(pick(before))[0]
        copies = [wire.put(block, block, me.along(axis, after))]
        down.wait_recv()
        block = halves(pick(after))[1]
        copies.append(wire.put(block, block, me.along(axis, before)))
    yield
    arrive(copies)


def reduce_ring(me, wire, axis, pick, far, near, out):
    t, n = me.mine(axis), me.side
    after, before = lax.rem(t + 1, n), lax.rem(t + n - 1, n)
    if n == 2:
        copies = [wire.put(pick(after), near.at[0], me.along(axis, after))]
    else:
        up, down = me.along(axis, after), me.along(axis, before)
        cross = halves(pick(lax.rem(t + 2, n)))
        to_up, to_down = halves(pick(after)), halves(pick(before))
        at_up, at_down = halves(near.at[0]), halves(near.at[1])
        first = [wire.put(cross[0], far.at[0], up), wire.put(cross[1], far.at[1], down)]
        copies = [wire.put(to_up[1], at_up[1], up), wire.put(to_down[0], at_down[0], down)]
        yield
        first[0].wait_recv()
        to_up[0][...] += far[0]
        copies.append(wire.put(to_up[0], at_up[0], up))
        first[1].wait_recv()
        to_down[1][...] += far[1]
        copies.append(wire.put(to_down[1], at_down[1], down))
    yield
    arrive(copies)
    out[...] = pick(t)[...] + near[0] if n == 2 else pick(t)[...] + near[0] + near[1]


def gather_direct(me, wire, axis, pick):
    mine = pick(me.mine(axis))
    copies = [wire.put(mine, mine, me.along(axis, t)) for _, t in me.others(axis)]
    yield
    arrive(copies)


def reduce_direct(me, wire, axis, pick, near, out):
    copies = [wire.put(pick(t), near.at[o - 1], me.along(axis, t)) for o, t in me.others(axis)]
    yield
    arrive(copies)
    total = pick(me.mine(axis))[...]
    for o in range(me.side - 1):
        total = total + near[o]
    out[...] = total


def together(*parts):
    parts = list(parts)
    while parts:
        for part in list(parts):
            if next(part, parts) is parts:
                parts.remove(part)


def arrive(copies):
    for copy in copies:
        copy.wait_recv()


def hops(depth, layer):
    far, near = depth // 2, depth - 1 - depth // 2
    return (far, near) if layer % 2 == 0 else (near, far)


def staged(parts):
    while parts:
        for part in list(parts):
            if next(part, parts) is parts:
                parts.remove(part)
        if parts:
            yield


def eye_block():
    row = lax.broadcasted_iota(jnp.int32, (NB, NB), 0)
    return (row == lax.broadcasted_iota(jnp.int32, (NB, NB), 1)).astype(F32)


def take_block(ref, n):
    piece, side = ref.shape[-2], ref.shape[1]
    parts, done = [], 0
    while done < NB:
        index, offset = (n * NB + done) // piece, (n * NB + done) % piece
        rows = min(piece - offset, NB - done)
        parts.append(ref[index // (side * side), index // side % side, index % side, offset : offset + rows])
        done += rows
    return jnp.concatenate(parts, axis=0)


def place_block(ref, n, block):
    piece = ref.shape[-2]
    flat, side = n * NB, ref.shape[1]
    done = 0
    while done < NB:
        index, offset = (flat + done) // piece, (flat + done) % piece
        rows = min(piece - offset, NB - done)
        ref[index // (side * side), index // side % side, index % side, offset : offset + rows] = block[done : done + rows]
        done += rows


def leaf_inverse(x):
    groups = NB // 8
    rows = [x[8 * g : 8 * g + 8, :] for g in range(groups)]
    lane = lax.broadcasted_iota(jnp.int32, (8, NB), 1)
    sub = lax.broadcasted_iota(jnp.int32, (8, NB), 0)
    splat = lambda v, p: jnp.broadcast_to(v[p : p + 1, :], (8, NB))
    out = []
    for g in range(groups):
        base = 8 * g
        inside = (lane >= base) & (lane < base + 8)
        cur = rows[g]
        cols = [jnp.broadcast_to(cur[:, base + q : base + q + 1], (8, NB)) for q in range(8)]
        fwd = jnp.where(inside, jnp.where(lane == sub + base, 1.0, 0.0), cur)
        full = fwd
        pivot = None
        for p in range(8):
            d = splat(cols[p], p)
            inv = 1.0 / d
            m = cols[p] * inv
            mf = jnp.where(sub > p, m, 0.0)
            mj = jnp.where(sub == p, 0.0, m)
            pivot = d if p == 0 else jnp.where(sub == p, d, pivot)
            ipivot = inv if p == 0 else jnp.where(sub == p, inv, ipivot)
            if p < 7:
                fwd = fwd - mf * splat(fwd, p)
            full = full - mj * splat(full, p)
            for q in range(p + 1, 8):
                cols[q] = cols[q] - mj * splat(cols[q], p)
        out.append(jnp.where(lane < base + 8, fwd * lax.rsqrt(pivot), 0.0))
        if g + 1 < groups:
            full = full * ipivot
            parts = [splat(full, q) for q in range(8)]
            for i in range(g + 1, groups):
                r = rows[i]
                acc = jnp.where(inside, 0.0, r)
                for q in range(8):
                    acc = acc - jnp.broadcast_to(r[:, base + q : base + q + 1], (8, NB)) * parts[q]
                rows[i] = acc
    return jnp.concatenate(out, axis=0)

def interleave(main, sides, every):
    count = 0
    for _ in main:
        count += 1
        if count % every == 0:
            for side in sides:
                next(side, None)
    for side in sides:
        for _ in side:
            pass


def dion_kernel(layers, side, depth, q_ref, m_hbm, all_ref, rb_ref, s_ref, new_ref, m_ref, qall, part, chain, p_ref, pcore, a_ref, near_a, b_ref, near_b, t_ref, s3, g_ref, wall, rt, rc, far1, near1, u, near2, tot, sq, sz, send, recv, load):
    me = Place(side, depth)
    wire = Wire(send, recv)
    x, y, c, z = me.x, me.y, me.c, me.z
    rank = p_ref.shape[-1]
    rows = part.shape[2]
    width = m_ref.shape[-1]
    blocks = rank // NB
    loads = [pltpu.make_async_copy(m_hbm.at[l], m_ref.at[l], load.at[l]) for l in range(layers)]
    for copy in loads:
        copy.start()
    qall[:, x, y, c] = q_ref[...]
    me.barrier()

    def factor_rows(l):
        yield from gather_direct(me, wire, l, lambda t: qall.at[l, t, y, c] if l == 0 else qall.at[l, x, t, c])
        yield from gather_direct(me, wire, 1 - l, lambda t: qall.at[l, :, t, c] if l == 0 else qall.at[l, t, :, c])
        crossing.append(wire.put(qall.at[l, :, :, c], qall.at[l, :, :, c], me.at(c=1 - c)))

    crossing = []
    together(*[factor_rows(l) for l in range(layers)])

    right, left = lax.rem(z + 1, depth), lax.rem(z + depth - 1, depth)

    def chain_step(l, way, s):
        count = hops(depth, l)[way]
        ahead = count - s + 1
        dest = lax.rem(z + ahead, depth) if way == 0 else lax.rem(z + depth - ahead, depth)
        src = part.at[l, dest]
        if s > 1:
            src = chain.at[l, way, s - 2]
            src[...] += part[l, dest]
        return wire.put(src, chain.at[l, way, s - 1], me.at(z=right if way == 0 else left))

    pending = {}
    for l in range(layers):
        crossing[l].wait_recv()
        loads[l].wait()
        factor = qall[l].reshape(rank, -1)

        @pl.loop(0, depth // 2)
        def _(i):
            lhs = m_ref[l, pl.ds(pl.multiple_of(i * 2 * rows, 16), 2 * rows), :]
            out = lax.dot_general(lhs, factor, (((1,), (1,)), ((), ())), preferred_element_type=F32)
            part[l, pl.ds(2 * i, 2)] = out.reshape(2, rows, rank)

        for way in (0, 1):
            if hops(depth, l)[way]:
                pending[l, way] = chain_step(l, way, 1)
    for s in range(2, depth // 2 + 1):
        for l in range(layers):
            for way in (0, 1):
                if s <= hops(depth, l)[way]:
                    pending[l, way].wait_recv()
                    pending[l, way] = chain_step(l, way, s)
    for l in range(layers):
        total = part[l, z]
        for way in (0, 1):
            count = hops(depth, l)[way]
            if count:
                pending[l, way].wait_recv()
                total = total + chain[l, way, count - 1]
        p_ref[l, z] = total

    def gather_project(l):
        pending = {}
        for s in range(1, depth // 2 + 1):
            for way in (0, 1):
                if s <= hops(depth, l)[way]:
                    if s > 1:
                        pending[way].wait_recv()
                    src = lax.rem(z + depth - (s - 1), depth) if way == 0 else lax.rem(z + s - 1, depth)
                    block = p_ref.at[l, src]
                    pending[way] = wire.put(block, block, me.at(z=right if way == 0 else left))
            yield
        arrive(list(pending.values()))

    def sum_plane(h):
        yield from reduce_direct(me, wire, h, lambda t: a_ref.at[h, t], near_a.at[h], b_ref.at[h])
        yield from reduce_direct(me, wire, 1 - h, lambda t: b_ref.at[h, t], near_b.at[h], t_ref.at[h])

    def spread_plane(h):
        i = me.mine(h)
        yield from gather_direct(me, wire, 1 - h, lambda t: g_ref.at[h, i, t])
        yield from gather_direct(me, wire, h, lambda t: g_ref.at[h, t])

    def sum_gram_and_invert():
        swap = wire.put(p_ref.at[1 - c, z], pcore, me.at(c=1 - c))
        for l in range(layers):
            next(sides[l])
        swap.wait_recv()
        both = jnp.concatenate([p_ref[c, z], pcore[...]], axis=0)
        n = 0
        for i in range(blocks):
            gram = lax.dot_general(both[:, i * NB : i * NB + NB], both[:, i * NB :], (((0,), (0,)), ((), ())), precision=HI, preferred_element_type=F32)
            for j in range(blocks - i):
                place_block(a_ref, n, gram[:, j * NB : j * NB + NB])
                n += 1
        yield from staged([sum_plane(0), sum_plane(1)])
        copies = [wire.put(t_ref, s3.at[o - 1], me.at(z=t)) for o, t in me.others_z()]
        yield
        arrive(copies)
        total = t_ref[...]
        for o in range(depth - 1):
            total = total + s3[o]
        for h in (0, 1):
            g_ref[h, me.mine(h), me.mine(1 - h)] = total[h]
        yield from staged([spread_plane(0), spread_plane(1)])
        wall[c] = jnp.zeros(wall.shape[1:], F32)
        n = 0
        for i in range(blocks):
            for j in range(i, blocks):
                wall[c, i * NB : i * NB + NB, j * NB : j * NB + NB] = take_block(g_ref, n)
                n += 1
        ident = eye_block()
        for k in range(blocks):
            yield
            sl = slice(k * NB, k * NB + NB)
            w = leaf_inverse(wall[c, sl, sl])
            colid = lax.broadcasted_iota(jnp.int32, (NB, rank), 1) // NB
            row = jnp.where(colid == k, jnp.concatenate([ident] * blocks, axis=1), wall[c, sl, :])
            out = jnp.dot(w, row, precision=HI, preferred_element_type=F32)
            wall[c, sl, :] = jnp.where(colid <= k, out, 0.0)
            if k + 1 < blocks:
                tail = slice(k * NB + NB, rank)
                upd = lax.dot_general(out[:, k * NB + NB :], out, (((0,), (0,)), ((), ())), precision=HI, preferred_element_type=F32)
                keep = wall[c, tail, :]
                cid = lax.broadcasted_iota(jnp.int32, keep.shape, 1) // NB
                wall[c, tail, :] = jnp.where(cid == k, 0.0, keep) - upd

    sides = [gather_project(l) for l in range(layers)]
    interleave(sum_gram_and_invert(), sides, 3)
    wire.put(wall.at[c], wall.at[c], me.at(c=1 - c)).wait_recv()

    def sum_rows(l):
        core = wire.put(rt.at[l, :, :, 1 - c], rc.at[l], me.at(c=1 - c))
        yield
        core.wait_recv()
        rc[l] += rt[l, :, :, c]
        pick = lambda t: rc.at[l, t] if l == 0 else rc.at[l, :, t]
        yield from reduce_ring(me, wire, l, pick, far1.at[l], near1.at[l], u.at[l])
        yield from reduce_direct(me, wire, 1 - l, lambda t: u.at[l, t], near2.at[l], tot.at[l])

    sums = []
    for l in range(layers):
        w_high = wall[l].astype(BF16)
        w_low = (wall[l] - w_high.astype(F32)).astype(BF16)

        @pl.loop(0, depth // 2)
        def _(i):
            lhs = p_ref[l, pl.ds(2 * i, 2)].reshape(-1, rank)
            high = lhs.astype(BF16)
            low = (lhs - high.astype(F32)).astype(BF16)
            dot = lambda a, b: lax.dot_general(a, b, (((1,), (1,)), ((), ())), preferred_element_type=F32)
            out = dot(high, w_high) + (dot(high, w_low) + dot(low, w_high))
            all_ref[l, pl.ds(2 * i, 2)] = out.astype(BF16).reshape(2, -1, rank)

        for part_sum in sums:
            next(part_sum)
        ortho = all_ref[l].reshape(-1, rank)
        for k in range(width // 256):
            cols = slice(256 * k, 256 * k + 256)
            out = lax.dot_general(ortho, m_ref[l, :, cols], (((0,), (0,)), ((), ())), preferred_element_type=F32)
            rt[l, :, :, :, :, cols] = out.reshape(rt.shape[1:5] + (256,))
        sums.append(sum_rows(l))
        next(sums[l])
    together(*sums)

    def gather_rows(l):
        rb_ref[l, x, y, c] = tot[l].astype(BF16)
        yield from gather_direct(me, wire, l, lambda t: rb_ref.at[l, t, y, c] if l == 0 else rb_ref.at[l, x, t, c])
        yield from gather_direct(me, wire, 1 - l, lambda t: rb_ref.at[l, :, t, c] if l == 0 else rb_ref.at[l, t, :, c])
        cross = wire.put(rb_ref.at[l, :, :, c], rb_ref.at[l, :, :, c], me.at(c=1 - c))
        yield
        cross.wait_recv()

    def gather_norms():
        for l in range(layers):
            sq[l] = jnp.broadcast_to(jnp.sum(tot[l] * tot[l], axis=1, keepdims=True), sq.shape[1:])
        copies = [wire.put(sq, sz.at[o - 1], me.at(z=t)) for o, t in me.others_z()]
        yield
        arrive(copies)
        norm = sq[...]
        for o in range(depth - 1):
            norm = norm + sz[o]
        factor = lax.rsqrt(norm + 1e-06)
        for l in range(layers):
            s_ref[l, x, y, c] = factor[l]
            new_ref[l] = (tot[l] * factor[l, :, :1]).astype(BF16)
        mine = s_ref.at[:, x, y, c]
        copies = [wire.put(mine, mine, me.along(0, t)) for _, t in me.others(0)]
        yield
        arrive(copies)
        mine = s_ref.at[:, :, y, c]
        copies = [wire.put(mine, mine, me.along(1, t)) for _, t in me.others(1)]
        yield
        arrive(copies)
        copies = [wire.put(s_ref.at[:, :, :, c], s_ref.at[:, :, :, c], me.at(c=1 - c))]
        yield
        arrive(copies)

    together(*[gather_rows(l) for l in range(layers)], gather_norms())
    wire.finish()


def dion(momentum, factor, side, depth):
    layers, rows, width = momentum.shape
    per = factor.shape[1]
    rank = per * side * side * CORES
    short = rows // depth
    blocks = rank // NB
    piece = blocks * (blocks + 1) // 2 * NB // (2 * side * side)
    whole = (2, side, side, piece, NB)
    grid = (side, side, CORES, per)
    ortho, rb, s, new = pl.pallas_call(
        functools.partial(dion_kernel, layers, side, depth),
        out_shape=(
            jax.ShapeDtypeStruct((layers, depth, short, rank), BF16),
            jax.ShapeDtypeStruct((layers,) + grid + (width,), BF16),
            jax.ShapeDtypeStruct((layers,) + grid + (128,), F32),
            jax.ShapeDtypeStruct((layers, per, width), BF16),
        ),
        in_specs=[pl.BlockSpec(memory_space=pltpu.VMEM), pl.BlockSpec(memory_space=pl.ANY)],
        out_specs=[pl.BlockSpec(memory_space=pltpu.VMEM)] * 4,
        scratch_shapes=[
            pltpu.VMEM(momentum.shape, BF16),
            pltpu.VMEM((layers,) + grid + (width,), BF16),
            pltpu.VMEM((layers, depth, short, rank), F32),
            pltpu.VMEM((layers, 2, max(1, depth // 2), short, rank), F32),
            pltpu.VMEM((layers, depth, short, rank), F32),
            pltpu.VMEM((short, rank), F32),
            pltpu.VMEM(whole, F32),
            pltpu.VMEM((2, side - 1) + whole[2:], F32),
            pltpu.VMEM((2,) + whole[2:], F32),
            pltpu.VMEM((2, side - 1) + whole[3:], F32),
            pltpu.VMEM((2,) + whole[3:], F32),
            pltpu.VMEM((depth - 1, 2) + whole[3:], F32),
            pltpu.VMEM(whole, F32),
            pltpu.VMEM((layers, rank, rank), F32),
            pltpu.VMEM((layers,) + grid + (width,), F32),
            pltpu.VMEM((layers, side, side, per, width), F32),
            pltpu.VMEM((layers, 2, side, per, width // 2), F32),
            pltpu.VMEM((layers, 2, side, per, width), F32),
            pltpu.VMEM((layers, side, per, width), F32),
            pltpu.VMEM((layers, side - 1, per, width), F32),
            pltpu.VMEM((layers, per, width), F32),
            pltpu.VMEM((layers, per, 128), F32),
            pltpu.VMEM((depth - 1, layers, per, 128), F32),
            pltpu.SemaphoreType.DMA((160,)),
            pltpu.SemaphoreType.DMA((160,)),
            pltpu.SemaphoreType.DMA((layers,)),
        ],
        compiler_params=pltpu.CompilerParams(collective_id=0, has_side_effects=True, vmem_limit_bytes=VMEM_BYTES),
        name="dion",
    )(factor, momentum)
    return ortho.reshape(layers, rows, rank), rb.reshape(layers, rank, width), s.reshape(layers, rank, 128), new


def final_kernel(scale, o_ref, m_ref, rb_ref, s_ref, mom_ref, up_ref):
    ortho, rb = o_ref[0], rb_ref[0]
    feedback = jnp.dot(ortho, rb, preferred_element_type=F32)
    mom_ref[0] = (m_ref[0].astype(F32) - 0.05 * feedback).astype(BF16)
    normed = (rb.astype(F32) * s_ref[0, :, :1]).astype(BF16)
    up_ref[0] = (scale * jnp.dot(ortho, normed, preferred_element_type=F32)).astype(BF16)


def final_products(ortho, momentum, rb, s, scale):
    layers, rows, rank = ortho.shape
    width = momentum.shape[-1]
    block = min(width, 256)
    cols = lambda n: pl.BlockSpec((1, n, block), lambda l, i: (l, 0, i))
    full = lambda n, w: pl.BlockSpec((1, n, w), lambda l, i: (l, 0, 0))
    return pl.pallas_call(
        functools.partial(final_kernel, scale),
        grid=(layers, width // block),
        out_shape=[jax.ShapeDtypeStruct(momentum.shape, BF16)] * 2,
        in_specs=[full(rows, rank), cols(rows), cols(rank), full(rank, 128)],
        out_specs=[cols(rows)] * 2,
        compiler_params=pltpu.CompilerParams(vmem_limit_bytes=VMEM_BYTES),
        name="final_products",
    )(ortho, momentum, rb, s)


def solution(mesh):
    side = math.isqrt(mesh.shape["fsdp"] // CORES)
    depth = mesh.shape["tp"]

    def local(momentum, right_factor):
        rank = right_factor.shape[1] * side * side * CORES
        total_rows, total_cols = momentum.shape[1] * side * side * CORES, momentum.shape[2] * depth
        scale = math.sqrt(total_rows * total_cols / rank)
        ortho, rb, s, new_factor = dion(momentum, right_factor, side, depth)
        new_momentum, update = final_products(ortho, momentum, rb, s, scale)
        return new_momentum, update, new_factor

    spec = P(None, "fsdp", "tp")
    return jax.shard_map(local, mesh=mesh, in_specs=(spec, spec), out_specs=(spec, spec, spec), check_vma=False)
```

time: 208 us -> 184 us (0.88)
  Pallas kernels: 204 us -> 181 us
    pallas_call x3 -> x1, Pallas kernels: 197 us -> 172 us  [dion(): pl.pallas_call(functools.partial(dion_kernel, layers, side, depth), out_s...]
where the time goes in v3:
time: 184 us; the launch traced here: 183 us
  Pallas kernels  181 us (98%)
    pallas_call x1, Pallas kernels, dion(): pl.pallas_call(functools.partial(dion_kernel, layers, side, depth), out_s...  172 us
    pallas_call x1, Pallas kernels, final_products(): pl.pallas_call(functools.partial(final_kernel, scale), grid=(layers, widt...  9.43 us

profile of v3, /device:TPU:1, one launch (start us, length us, event | category | flops | bytes accessed | tf_op | source)
XLA Modules:
  0.0 183.4 jit_solution(6495247377721559653)
XLA Ops:
  0.6 0.0 copy-start
  0.6 0.8 copy-done
  1.5 171.9 %dion.1 = (bf16[2,8,112,512]{3,2,1,0:T(8,128)(2,1)S(1)}, bf16[2,4,4,2,16,1024]{5,4,3,2,1,0:T(8,128)(2,1)S(1)}, f32[2,4,4,2,16,128]{5,4,3,2,1,0:T(8,128)S(1)}, bf16[2,16,1024]{2,1,0:T(8,128)(2,1)S(1)}) custom-call(bf16[2,16,1024]{2,1,0:T(8,128)(2,1)S(1)} %copy-done, bf16[2,896,1024]{2,1,0:T(8,128)(2,1)} %m_ref.1), custom_call_target="tpu_custom_call" | custom-call | tf_op jit(solution)/shard_map/dion/pallas_call | solution.py:465
  173.4 9.4 %final_products.1 = (bf16[2,896,1024]{2,1,0:T(8,128)(2,1)}, bf16[2,896,1024]{2,1,0:T(8,128)(2,1)}) custom-call(bf16[2,896,512]{2,1,0:T(8,128)(2,1)S(1)} %bitcast.4, bf16[2,896,1024]{2,1,0:T(8,128)(2,1)} %m_ref.1, bf16[2,512,1024]{2,1,0:T(8,128)(2,1)S(1)} %bitcast.3, f32[2,512,128]{2,1,0:T(8,128)S(1)} %bitcast.5), custom_call_target="tpu_custom_call" | custom-call | tf_op jit(solution)/shard_map/final_products/pallas_call | solution.py:523
  182.8 0.6 copy.6
Async XLA Ops:
  0.6 0.8 copy-start

commit v4 on v3

--- a/solution.py
+++ b/solution.py
@@ -12,6 +12,7 @@
 HI = lax.Precision.HIGHEST
 CORES = 2
 NB = 128
+SPAN = 4
 VMEM_BYTES = 48 * 2**20
 F32 = jnp.float32
 BF16 = jnp.bfloat16
@@ -210,37 +211,49 @@
         cols = [jnp.broadcast_to(cur[:, base + q : base + q + 1], (8, NB)) for q in range(8)]
         fwd = jnp.where(inside, jnp.where(lane == sub + base, 1.0, 0.0), cur)
         full = fwd
-        pivot = None
+        last = (g + 1) % SPAN == 0
         for p in range(8):
             d = splat(cols[p], p)
             inv = 1.0 / d
             m = cols[p] * inv
             mf = jnp.where(sub > p, m, 0.0)
-            mj = jnp.where(sub == p, 0.0, m)
             pivot = d if p == 0 else jnp.where(sub == p, d, pivot)
             ipivot = inv if p == 0 else jnp.where(sub == p, inv, ipivot)
             if p < 7:
                 fwd = fwd - mf * splat(fwd, p)
-            full = full - mj * splat(full, p)
+            if not last:
+                mj = jnp.where(sub == p, 0.0, m)
+                full = full - mj * splat(full, p)
             for q in range(p + 1, 8):
-                cols[q] = cols[q] - mj * splat(cols[q], p)
-        out.append(jnp.where(lane < base + 8, fwd * lax.rsqrt(pivot), 0.0))
-        if g + 1 < groups:
+                cols[q] = cols[q] - (mf if last else mj) * splat(cols[q], p)
+        y = fwd * lax.rsqrt(pivot)
+        out.append(y)
+        if last:
+            if g + 1 < groups:
+                first = g + 1 - SPAN
+                block = jnp.concatenate(out[first : g + 1], axis=0)
+                right = jnp.concatenate([jnp.where((lane >= 8 * f + 8) & (lane < base + 8), 0.0, out[f]) for f in range(first, g + 1)], axis=0)
+                upd = lax.dot_general(block, right, (((0,), (0,)), ((), ())), precision=HI, preferred_element_type=F32)
+                gone = (lane >= 8 * first) & (lane < base + 8)
+                for i in range(g + 1, groups):
+                    rows[i] = jnp.where(gone, 0.0, rows[i]) - upd[8 * i : 8 * i + 8, :]
+        else:
             full = full * ipivot
             parts = [splat(full, q) for q in range(8)]
-            for i in range(g + 1, groups):
+            for i in range(g + 1, g + 1 - (g + 1) % SPAN + SPAN):
                 r = rows[i]
                 acc = jnp.where(inside, 0.0, r)
                 for q in range(8):
                     acc = acc - jnp.broadcast_to(r[:, base + q : base + q + 1], (8, NB)) * parts[q]
                 rows[i] = acc
-    return jnp.concatenate(out, axis=0)
-
-def interleave(main, sides, every):
+    return jnp.concatenate([jnp.where(lane < 8 * g + 8, y, 0.0) for g, y in enumerate(out)], axis=0)
+
+
+def interleave(main, sides, turns):
     count = 0
     for _ in main:
         count += 1
-        if count % every == 0:
+        if count in turns:
             for side in sides:
                 next(side, None)
     for side in sides:
@@ -248,7 +261,7 @@
             pass
 
 
-def dion_kernel(layers, side, depth, q_ref, m_hbm, all_ref, rb_ref, s_ref, new_ref, m_ref, qall, part, chain, p_ref, pcore, a_ref, near_a, b_ref, near_b, t_ref, s3, g_ref, wall, rt, rc, far1, near1, u, near2, tot, sq, sz, send, recv, load):
+def dion_kernel(layers, side, depth, q_ref, m_hbm, all_ref, rb_ref, s_ref, new_ref, m_ref, qall, part, chain, p_ref, pcore, a_ref, near_a, b_ref, near_b, t_ref, s3, g_ref, wall, rt, rc, far1, near1, u, near2, tot, sq, sz, qt, wt, send, recv, load):
     me = Place(side, depth)
     wire = Wire(send, recv)
     x, y, c, z = me.x, me.y, me.c, me.z
@@ -286,12 +299,12 @@
     for l in range(layers):
         crossing[l].wait_recv()
         loads[l].wait()
-        factor = qall[l].reshape(rank, -1)
+        qt[...] = jnp.transpose(qall[l].reshape(rank, -1))
 
         @pl.loop(0, depth // 2)
         def _(i):
             lhs = m_ref[l, pl.ds(pl.multiple_of(i * 2 * rows, 16), 2 * rows), :]
-            out = lax.dot_general(lhs, factor, (((1,), (1,)), ((), ())), preferred_element_type=F32)
+            out = jnp.dot(lhs, qt[...], preferred_element_type=F32)
             part[l, pl.ds(2 * i, 2)] = out.reshape(2, rows, rank)
 
         for way in (0, 1):
@@ -379,7 +392,7 @@
                 wall[c, tail, :] = jnp.where(cid == k, 0.0, keep) - upd
 
     sides = [gather_project(l) for l in range(layers)]
-    interleave(sum_gram_and_invert(), sides, 3)
+    interleave(sum_gram_and_invert(), sides, (3, 5, 7))
     wire.put(wall.at[c], wall.at[c], me.at(c=1 - c)).wait_recv()
 
     def sum_rows(l):
@@ -393,16 +406,17 @@
 
     sums = []
     for l in range(layers):
-        w_high = wall[l].astype(BF16)
-        w_low = (wall[l] - w_high.astype(F32)).astype(BF16)
+        turned = jnp.transpose(wall[l])
+        wt[0] = turned.astype(BF16)
+        wt[1] = (turned - turned.astype(BF16).astype(F32)).astype(BF16)
 
         @pl.loop(0, depth // 2)
         def _(i):
             lhs = p_ref[l, pl.ds(2 * i, 2)].reshape(-1, rank)
             high = lhs.astype(BF16)
             low = (lhs - high.astype(F32)).astype(BF16)
-            dot = lambda a, b: lax.dot_general(a, b, (((1,), (1,)), ((), ())), preferred_element_type=F32)
-            out = dot(high, w_high) + (dot(high, w_low) + dot(low, w_high))
+            dot = lambda a, b: jnp.dot(a, b, preferred_element_type=F32)
+            out = dot(high, wt[0]) + (dot(high, wt[1]) + dot(low, wt[0]))
             all_ref[l, pl.ds(2 * i, 2)] = out.astype(BF16).reshape(2, -1, rank)
 
         for part_sum in sums:
@@ -496,6 +510,8 @@
             pltpu.VMEM((layers, per, width), F32),
             pltpu.VMEM((layers, per, 128), F32),
             pltpu.VMEM((depth - 1, layers, per, 128), F32),
+            pltpu.VMEM((width, rank), BF16),
+            pltpu.VMEM((2, rank, rank), BF16),
             pltpu.SemaphoreType.DMA((160,)),
             pltpu.SemaphoreType.DMA((160,)),
             pltpu.SemaphoreType.DMA((layers,)),
@@ -517,15 +533,15 @@
 def final_products(ortho, momentum, rb, s, scale):
     layers, rows, rank = ortho.shape
     width = momentum.shape[-1]
-    block = min(width, 256)
-    cols = lambda n: pl.BlockSpec((1, n, block), lambda l, i: (l, 0, i))
-    full = lambda n, w: pl.BlockSpec((1, n, w), lambda l, i: (l, 0, 0))
+    block = rows // 2
+    tall = lambda w: pl.BlockSpec((1, block, w), lambda l, i: (l, i, 0))
+    full = lambda w: pl.BlockSpec((1, rank, w), lambda l, i: (l, 0, 0))
     return pl.pallas_call(
         functools.partial(final_kernel, scale),
-        grid=(layers, width // block),
+        grid=(layers, 2),
         out_shape=[jax.ShapeDtypeStruct(momentum.shape, BF16)] * 2,
-        in_specs=[full(rows, rank), cols(rows), cols(rank), full(rank, 128)],
-        out_specs=[cols(rows)] * 2,
+        in_specs=[tall(rank), tall(width), full(width), full(128)],
+        out_specs=[tall(width)] * 2,
         compiler_params=pltpu.CompilerParams(vmem_limit_bytes=VMEM_BYTES),
         name="final_products",
     )(ortho, momentum, rb, s)

time: 184 us -> 180 us (0.978)
  Pallas kernels: 181 us -> 178 us
    pallas_call x1, Pallas kernels: 9.43 us -> 7.15 us  [final_products(): pl.pallas_call(functools.partial(final_kernel, scale), grid=(layers, 2),...]
where the time goes in v4:
time: 180 us
  Pallas kernels  178 us (99%)
    pallas_call x1, Pallas kernels, dion(): pl.pallas_call(functools.partial(dion_kernel, layers, side, depth), out_s...  171 us
    pallas_call x1, Pallas kernels, final_products(): pl.pallas_call(functools.partial(final_kernel, scale), grid=(layers, 2),...  7.15 us

profile of v4, /device:TPU:1, one launch (start us, length us, event | category | flops | bytes accessed | tf_op | source)
XLA Modules:
  0.0 179.8 jit_solution(14193919471508521266)
XLA Ops:
  0.6 0.0 copy-start
  0.6 0.8 copy-done
  1.5 170.5 %dion.1 = (bf16[2,8,112,512]{3,2,1,0:T(8,128)(2,1)S(1)}, bf16[2,4,4,2,16,1024]{5,4,3,2,1,0:T(8,128)(2,1)S(1)}, f32[2,4,4,2,16,128]{5,4,3,2,1,0:T(8,128)S(1)}, bf16[2,16,1024]{2,1,0:T(8,128)(2,1)S(1)}) custom-call(bf16[2,16,1024]{2,1,0:T(8,128)(2,1)S(1)} %copy-done, bf16[2,896,1024]{2,1,0:T(8,128)(2,1)} %m_ref.1), custom_call_target="tpu_custom_call" | custom-call | tf_op jit(solution)/shard_map/dion/pallas_call | solution.py:479
  172.0 7.2 %final_products.1 = (bf16[2,896,1024]{2,1,0:T(8,128)(2,1)}, bf16[2,896,1024]{2,1,0:T(8,128)(2,1)}) custom-call(bf16[2,896,512]{2,1,0:T(8,128)(2,1)S(1)} %bitcast.4, bf16[2,896,1024]{2,1,0:T(8,128)(2,1)} %m_ref.1, bf16[2,512,1024]{2,1,0:T(8,128)(2,1)S(1)} %bitcast.3, f32[2,512,128]{2,1,0:T(8,128)S(1)} %bitcast.5), custom_call_target="tpu_custom_call" | custom-call | tf_op jit(solution)/shard_map/final_products/pallas_call | solution.py:539
  179.2 0.6 copy.6
Async XLA Ops:
  0.6 0.8 copy-start

commit v5 on v4

--- a/solution.py
+++ b/solution.py
@@ -463,7 +463,7 @@
         yield
         arrive(copies)
 
-    together(*[gather_rows(l) for l in range(layers)], gather_norms())
+    together(gather_norms(), *[gather_rows(l) for l in range(layers)])
     wire.finish()
 
 

time: 180 us -> 180 us (level)
  no operation moved by 1% of the time
where the time goes in v5:
time: 180 us
  Pallas kernels  178 us (99%)
    pallas_call x1, Pallas kernels, dion(): pl.pallas_call(functools.partial(dion_kernel, layers, side, depth), out_s...  170 us
    pallas_call x1, Pallas kernels, final_products(): pl.pallas_call(functools.partial(final_kernel, scale), grid=(layers, 2),...  7.15 us

profile of v5, /device:TPU:1, one launch (start us, length us, event | category | flops | bytes accessed | tf_op | source)
XLA Modules:
  0.0 179.7 jit_solution(3247619851079920507)
XLA Ops:
  0.6 0.0 copy-start
  0.6 0.8 copy-done
  1.5 170.4 %dion.1 = (bf16[2,8,112,512]{3,2,1,0:T(8,128)(2,1)S(1)}, bf16[2,4,4,2,16,1024]{5,4,3,2,1,0:T(8,128)(2,1)S(1)}, f32[2,4,4,2,16,128]{5,4,3,2,1,0:T(8,128)S(1)}, bf16[2,16,1024]{2,1,0:T(8,128)(2,1)S(1)}) custom-call(bf16[2,16,1024]{2,1,0:T(8,128)(2,1)S(1)} %copy-done, bf16[2,896,1024]{2,1,0:T(8,128)(2,1)} %m_ref.1), custom_call_target="tpu_custom_call" | custom-call | tf_op jit(solution)/shard_map/dion/pallas_call | solution.py:479
  171.9 7.2 %final_products.1 = (bf16[2,896,1024]{2,1,0:T(8,128)(2,1)}, bf16[2,896,1024]{2,1,0:T(8,128)(2,1)}) custom-call(bf16[2,896,512]{2,1,0:T(8,128)(2,1)S(1)} %bitcast.4, bf16[2,896,1024]{2,1,0:T(8,128)(2,1)} %m_ref.1, bf16[2,512,1024]{2,1,0:T(8,128)(2,1)S(1)} %bitcast.3, f32[2,512,128]{2,1,0:T(8,128)S(1)} %bitcast.5), custom_call_target="tpu_custom_call" | custom-call | tf_op jit(solution)/shard_map/final_products/pallas_call | solution.py:539
  179.0 0.6 copy.6
Async XLA Ops:
  0.6 0.8 copy-start
